TPU v7x, 512 devices: a whole 4x8x8 slice. The times are simulated.
512 devices in a mesh: blk: 64 (over y_lo, z, core), uly: 8 (over x, y_hi).
Axes of the slice: x: 4, y: 8 (y_hi: 2, y_lo: 4; y = y_hi * 4 + y_lo), z: 8, core: 2. Of those that a mesh axis runs over, the one named last changes fastest.
Arguments:
- queries: bfloat16 [36864, 3072], P(('blk', 'uly')), may hold values from -17.5 to 17.5
- keys: bfloat16 [36864, 3072], P(('blk', 'uly')), may hold values from -10.2 to 10.2
- values: bfloat16 [36864, 3072], P(('blk', 'uly')), may hold values from -6 to 6
- tile_pairs: int32 [192, 8], replicated, may hold values from 0 to 191, as said below
- tile_coords: int32 [192, 3], replicated, may hold values from 0 to 31, as said below
Outputs:
- attended: bfloat16 [36864, 3072], P(('blk', 'uly'))
Inputs may be any that keep to these rules, and one draw needn't show every extreme that they name: Tile index t stands for the grid cell (t % 2, (t // 2) % 3, t // 6); tile_pairs[t] lists the 8 distinct tiles of a block of 2 frames x 2 rows x 2 columns of cells that holds tile t's cell; every listed tile lies within 9 positions of t in the tile order, and that distance is reached. tile_coords gives every cell of the 2 x 3 x 32 tile grid once: tile t's cell as in tile_pairs, each of the three coordinates possibly mirrored over the whole grid.
All inputs are finite; a program needn't handle non-finite values.
Results may differ from a plain program's by a relative error of at most 0.009.
Values may be sent and summed in bfloat16 or wider, within the bound.
A program may use at most 64 MiB of HBM per device.

v0:
```python
import math

import jax
import jax.numpy as jnp
from jax import lax
from jax.sharding import PartitionSpec as P

HEAD_DIM = 128
TF = 3
TH = 8
TW = 8
GF = 2
GH = 3
KPT = 8
TILE = 192


def shifted(value, axis, steps):
    count = lax.axis_size(axis)
    leading, last = (max(0, -steps), min(count, count - steps))
    return lax.ppermute(value, axis, [(source, source + steps) for source in range(leading, last)])


def rope_angles(coords):
    offset = jnp.arange(TILE, dtype=jnp.int32)
    frame_pos = (coords[:, 0:1] * TF + offset[None, :] // (TH * TW)).astype(jnp.float32)
    height_pos = (coords[:, 1:2] * TH + offset[None, :] // TW % TH).astype(jnp.float32)
    width_pos = (coords[:, 2:3] * TW + offset[None, :] % TW).astype(jnp.float32)
    halves = HEAD_DIM // 2
    side_pairs = HEAD_DIM // 6
    frame_pairs = halves - 2 * side_pairs
    pair_index = jnp.arange(halves, dtype=jnp.int32)
    within = jnp.where(
        pair_index < frame_pairs,
        pair_index,
        jnp.where(
            pair_index < frame_pairs + side_pairs,
            pair_index - frame_pairs,
            pair_index - frame_pairs - side_pairs,
        ),
    ).astype(jnp.float32)
    axis_len = jnp.where(pair_index < frame_pairs, frame_pairs, side_pairs).astype(jnp.float32)
    frequency = jnp.exp(-math.log(10000.0) * within / axis_len)
    angles = jnp.where(
        pair_index < frame_pairs,
        frame_pos[..., None] * frequency,
        jnp.where(
            pair_index < frame_pairs + side_pairs,
            height_pos[..., None] * frequency,
            width_pos[..., None] * frequency,
        ),
    )
    return (jnp.cos(angles), jnp.sin(angles))


def rotate(tensor, cosine_table, sine_table):
    halves = HEAD_DIM // 2
    first_half = tensor[..., :halves].astype(jnp.float32)
    second_half = tensor[..., halves:].astype(jnp.float32)
    cosine_part = cosine_table[:, :, None, :]
    sine_part = sine_table[:, :, None, :]
    joined = jnp.concatenate(
        (
            first_half * cosine_part - second_half * sine_part,
            first_half * sine_part + second_half * cosine_part,
        ),
        axis=-1,
    )
    return joined.astype(jnp.bfloat16)


def attend(query_tile, key_rows, value_rows):
    scaling = HEAD_DIM ** (-0.5)
    scores = (
        jnp.einsum("qhd,khd->hqk", query_tile, key_rows, preferred_element_type=jnp.float32)
        * scaling
    )
    row_max = jnp.max(scores, axis=2, keepdims=True)
    weights = jnp.exp(scores - row_max)
    row_total = jnp.sum(weights, axis=2, keepdims=True)
    rounded = weights.astype(jnp.bfloat16)
    summed = jnp.einsum("hqk,khd->qhd", rounded, value_rows, preferred_element_type=jnp.float32)
    result = (summed / jnp.transpose(row_total, (1, 0, 2))).astype(jnp.bfloat16)
    return result.reshape(query_tile.shape[0], -1)


def on_device(queries, keys, values, tile_pairs, tile_coords):
    head_q, head_k, head_v = (
        lax.all_to_all(queries, "uly", split_axis=1, concat_axis=0, tiled=True),
        lax.all_to_all(keys, "uly", split_axis=1, concat_axis=0, tiled=True),
        lax.all_to_all(values, "uly", split_axis=1, concat_axis=0, tiled=True),
    )
    row_count = head_k.shape[0]
    columns = head_k.shape[1]
    heads_here = columns // HEAD_DIM
    tiles_here = row_count // TILE
    reach_shards = (tiles_here + GF * GH + GF) // tiles_here
    block_index = lax.axis_index("blk")
    first_tile = block_index * tiles_here
    coords = lax.dynamic_slice_in_dim(tile_coords, first_tile, tiles_here, 0)
    cosine_table, sine_table = rope_angles(coords)
    grid_shape = (tiles_here, TILE, heads_here, HEAD_DIM)
    rotated_k = rotate(head_k.reshape(grid_shape), cosine_table, sine_table).reshape(
        row_count, columns
    )
    paired = jnp.stack((rotated_k, head_v))
    lower_parts = []
    upper_parts = []
    moving_down = paired
    moving_up = paired
    for distance in range(reach_shards):
        moving_down = shifted(moving_down, "blk", 1)
        moving_up = shifted(moving_up, "blk", -1)
        lower_parts.append(moving_down)
        upper_parts.append(moving_up)
    window = jnp.concatenate(lower_parts[::-1] + [paired] + upper_parts, axis=1)
    window = window.reshape(2, (2 * reach_shards + 1) * tiles_here, TILE, columns)
    rotated_q = rotate(head_q.reshape(grid_shape), cosine_table, sine_table)
    listed = (
        lax.dynamic_slice_in_dim(tile_pairs, first_tile, tiles_here, 0)
        - (block_index - reach_shards) * tiles_here
    )

    def one_tile(inputs):
        query_tile, chosen = inputs
        picked = jnp.take(window, chosen, axis=1).reshape(2, KPT * TILE, heads_here, HEAD_DIM)
        return attend(query_tile, picked[0], picked[1])

    attended = lax.map(one_tile, (rotated_q, listed))
    return lax.all_to_all(
        attended.reshape(row_count, columns), "uly", split_axis=0, concat_axis=1, tiled=True
    )


def solution(mesh):
    return jax.shard_map(
        on_device,
        mesh=mesh,
        in_specs=(
            P(("blk", "uly"), None),
            P(("blk", "uly"), None),
            P(("blk", "uly"), None),
            P(),
            P(),
        ),
        out_specs=P(("blk", "uly"), None),
        check_vma=False,
    )
```

profile of v0, /device:TPU:16, one launch (start us, length us, event | category | flops | bytes accessed | tf_op | source)
XLA Modules:
  0.0 199.1 jit_solution(16507439493673524205)
XLA Ops:
  0.0 1.8 copy.91
  1.8 7.8 %all-to-all-start = ((bf16[72,8,384]{2,0,1:T(8,128)(2,1)}), bf16[72,8,384]{2,0,1:T(8,128)(2,1)S(1)}, u32[]{:S(2)}, u32[]{:S(2)}) async-start(bf16[72,8,384]{2,0,1:T(8,128)(2,1)} %bitcast.59), calls=%async_computation | async-start | bytes 884736 | tf_op jit(solution)/shard_map/all_to_all | solution.py:90
  9.6 1.8 copy.89
  13.4 14.1 %all-to-all-done = bf16[72,8,384]{2,0,1:T(8,128)(2,1)S(1)} async-done(((bf16[72,8,384]{2,0,1:T(8,128)(2,1)}), bf16[72,8,384]{2,0,1:T(8,128)(2,1)S(1)}, u32[]{:S(2)}, u32[]{:S(2)}) %all-to-all-start) | async-done | bytes 442400 | tf_op jit(solution)/shard_map/all_to_all | solution.py:90
  27.5 3.5 %all-to-all-start.2 = ((bf16[72,8,384]{2,0,1:T(8,128)(2,1)}), bf16[72,8,384]{2,0,1:T(8,128)(2,1)S(1)}, u32[]{:S(2)}, u32[]{:S(2)}) async-start(bf16[72,8,384]{2,0,1:T(8,128)(2,1)} %bitcast.57), calls=%async_computation.2 | async-start | bytes 884736 | tf_op jit(solution)/shard_map/all_to_all | solution.py:89
  32.7 12.1 %all-to-all-done.2 = bf16[72,8,384]{2,0,1:T(8,128)(2,1)S(1)} async-done(((bf16[72,8,384]{2,0,1:T(8,128)(2,1)}), bf16[72,8,384]{2,0,1:T(8,128)(2,1)S(1)}, u32[]{:S(2)}, u32[]{:S(2)}) %all-to-all-start.2) | async-done | bytes 442400 | tf_op jit(solution)/shard_map/all_to_all | solution.py:89
  44.9 3.5 %all-to-all-start.1 = ((bf16[72,8,384]{2,0,1:T(8,128)(2,1)}), bf16[72,8,384]{2,0,1:T(8,128)(2,1)S(1)}, u32[]{:S(2)}, u32[]{:S(2)}) async-start(bf16[72,8,384]{2,0,1:T(8,128)(2,1)} %bitcast.58), calls=%async_computation.1 | async-start | bytes 884736 | tf_op jit(solution)/shard_map/all_to_all | solution.py:91
  53.6 8.5 %all-to-all-done.1 = bf16[72,8,384]{2,0,1:T(8,128)(2,1)S(1)} async-done(((bf16[72,8,384]{2,0,1:T(8,128)(2,1)}), bf16[72,8,384]{2,0,1:T(8,128)(2,1)S(1)}, u32[]{:S(2)}, u32[]{:S(2)}) %all-to-all-start.1) | async-done | bytes 442400 | tf_op jit(solution)/shard_map/all_to_all | solution.py:91
  62.2 1.9 collective-permute-start
  64.1 11.4 %collective-permute-start.3 = (bf16[2,576,384]{2,1,0:T(8,128)(2,1)S(1)}, bf16[2,576,384]{2,1,0:T(8,128)(2,1)S(1)}, u32[]{:S(2)}, u32[]{:S(2)}) collective-permute-start(bf16[2,576,384]{2,1,0:T(8,128)(2,1)S(1)} %pad_maximum_fusion), channel_id=1, source_target_pairs={{8,0},{16,8},{24,16},{32,24},{40,32},{48,40},{56,48},{64,56},{72,6... | collective-permute-start | bytes 2654216 | tf_op jit(solution)/shard_map/ppermute | solution.py:21
  75.5 8.8 %collective-permute-done = bf16[2,576,384]{2,1,0:T(8,128)(2,1)S(1)} collective-permute-done((bf16[2,576,384]{2,1,0:T(8,128)(2,1)S(1)}, bf16[2,576,384]{2,1,0:T(8,128)(2,1)S(1)}, u32[]{:S(2)}, u32[]{:S(2)}) %collective-permute-start) | collective-permute-done | bytes 884768 | tf_op jit(solution)/shard_map/ppermute | solution.py:21
  84.3 1.9 collective-permute-start.1
  86.2 5.8 %collective-permute-start.4 = (bf16[2,576,384]{2,1,0:T(8,128)(2,1)S(1)}, bf16[2,576,384]{2,1,0:T(8,128)(2,1)}, u32[]{:S(2)}, u32[]{:S(2)}) collective-permute-start(bf16[2,576,384]{2,1,0:T(8,128)(2,1)S(1)} %collective-permute-done.3), channel_id=1, source_target_pairs={{8,0},{16,8},{24,16},{32,24},{40,32},{48,40},{56,48},{64,56},{72,6... | collective-permute-start | bytes 2654216 | tf_op jit(solution)/shard_map/ppermute | solution.py:21
  92.0 8.9 %collective-permute-done.1 = bf16[2,576,384]{2,1,0:T(8,128)(2,1)} collective-permute-done((bf16[2,576,384]{2,1,0:T(8,128)(2,1)S(1)}, bf16[2,576,384]{2,1,0:T(8,128)(2,1)}, u32[]{:S(2)}, u32[]{:S(2)}) %collective-permute-start.1) | collective-permute-done | bytes 884768 | tf_op jit(solution)/shard_map/ppermute | solution.py:21
  100.9 1.9 collective-permute-start.2
  103.6 5.7 %collective-permute-start.5 = (bf16[2,576,384]{2,1,0:T(8,128)(2,1)}, bf16[2,576,384]{2,1,0:T(8,128)(2,1)}, u32[]{:S(2)}, u32[]{:S(2)}) collective-permute-start(bf16[2,576,384]{2,1,0:T(8,128)(2,1)} %collective-permute-done.4), channel_id=1, source_target_pairs={{8,0},{16,8},{24,16},{32,24},{40,32},{48,40},{56,48},{64,56},{72,6... | collective-permute-start | bytes 2654216 | tf_op jit(solution)/shard_map/ppermute | solution.py:21
  110.4 7.2 %collective-permute-done.2 = bf16[2,576,384]{2,1,0:T(8,128)(2,1)} collective-permute-done((bf16[2,576,384]{2,1,0:T(8,128)(2,1)}, bf16[2,576,384]{2,1,0:T(8,128)(2,1)}, u32[]{:S(2)}, u32[]{:S(2)}) %collective-permute-start.2) | collective-permute-done | bytes 884768 | tf_op jit(solution)/shard_map/ppermute | solution.py:21
  123.5 2.6 %copy-done.1 = bf16[2,4032,384]{2,1,0:T(8,128)(2,1)} copy-done((bf16[2,4032,384]{2,1,0:T(8,128)(2,1)}, bf16[2,4032,384]{2,1,0:T(8,128)(2,1)S(1)}, u32[]{:S(2)}) %copy-start.1) | copy-done | bytes 6193176
  126.1 56.6 %while.10 = (s32[]{:T(128)}, bf16[3,192,384]{2,1,0:T(8,128)(2,1)}, s32[3,8]{1,0:T(4,128)}, bf16[2,21,192,384]{3,2,1,0:T(8,128)(2,1)}, bf16[3,192,3,128]{3,1,2,0:T(8,128)(2,1)}, /*index=5*/s32[]{:T(128)}) while((s32[]{:T(128)}, bf16[3,192,384]{2,1,0:T(8,128)(2,1)}, s32[3,8]{1,0:T(4,128)}, bf16[2,21,192,384]{3,2,1,0:T(8,128)(2,1)}, ...), condition=%wide.region_3.4_spmd, body=%wide.region_0.3_spmd.sunk | while | flops 459620288 | bytes 33440252 | solution.py:129
  126.8 3.8 %gather_fusion = bf16[8,2,192,384]{3,2,1,0:T(8,128)(2,1)S(1)} fusion(bf16[2,21,192,384]{3,2,1,0:T(8,128)(2,1)} %get-tuple-element.140, s32[1024]{0:T(1024)S(1)} %pad_clamp_fusion.2), kind=kCustom, calls=%fused_computation.clone.1 | custom fusion | bytes 4718624 | tf_op jit(solution)/shard_map/while/body/eval_jaxpr/jit(_take)/gather | solution.py:126
  134.8 2.2 %fusion.56 = (f32[3,192]{1,0:T(4,128)S(1)}, f32[3,192,1536]{2,1,0:T(8,128)S(1)}) fusion(bf16[1536,3,128]{2,1,0:T(4,128)(2,1)} %reshape.316, bf16[3,192,3,128]{3,1,2,0:T(8,128)(2,1)} %get-tuple-element.141, s32[]{:T(128)} %get-tuple-element.131), kind=kOutput, calls=%fused_computation.87.clone.1 | convolution fusion | flops 228261312 | bytes 5262080 | tf_op jit(solution)/shard_map/while/body/eval_jaxpr/qhd,khd->hqk/dot_general | solution.py:75
  137.7 4.1 %reshape.315 = bf16[1536,3,128]{2,1,0:T(4,128)(2,1)} reshape(bf16[1,8,192,384]{3,2,0,1:T(8,128)(2,1)} %get-tuple-element.121) | data formatting | bytes 2359296 | tf_op jit(solution)/shard_map/while/body/eval_jaxpr/squeeze | solution.py:127
  141.7 2.3 %fusion.58 = bf16[192,3,128]{2,0,1:T(8,128)(2,1)S(1)} fusion(bf16[1536,3,128]{2,1,0:T(4,128)(2,1)} %reshape.315, f32[3,192,1536]{2,1,0:T(8,128)S(1)} %get-tuple-element.123, f32[3,192]{1,0:T(4,128)S(1)} %get-tuple-element.124, f32[192,3]{0,1:T(4,128)S(1)} %bitcast.84), kind=kOutput, calls=%fused_computation.12.clone.1 | convolution fusion | flops 228409344 | bytes 4870656 | tf_op jit(solution)/shard_map/while/body/eval_jaxpr/hqk,khd->qhd/dot_general | solution.py:82
  145.7 3.8 %gather_fusion = bf16[8,2,192,384]{3,2,1,0:T(8,128)(2,1)S(1)} fusion(bf16[2,21,192,384]{3,2,1,0:T(8,128)(2,1)} %get-tuple-element.140, s32[1024]{0:T(1024)S(1)} %pad_clamp_fusion.2), kind=kCustom, calls=%fused_computation.clone.1 | custom fusion | bytes 4718624 | tf_op jit(solution)/shard_map/while/body/eval_jaxpr/jit(_take)/gather | solution.py:126
  153.6 2.2 %fusion.56 = (f32[3,192]{1,0:T(4,128)S(1)}, f32[3,192,1536]{2,1,0:T(8,128)S(1)}) fusion(bf16[1536,3,128]{2,1,0:T(4,128)(2,1)} %reshape.316, bf16[3,192,3,128]{3,1,2,0:T(8,128)(2,1)} %get-tuple-element.141, s32[]{:T(128)} %get-tuple-element.131), kind=kOutput, calls=%fused_computation.87.clone.1 | convolution fusion | flops 228261312 | bytes 5262080 | tf_op jit(solution)/shard_map/while/body/eval_jaxpr/qhd,khd->hqk/dot_general | solution.py:75
  156.5 4.1 %reshape.315 = bf16[1536,3,128]{2,1,0:T(4,128)(2,1)} reshape(bf16[1,8,192,384]{3,2,0,1:T(8,128)(2,1)} %get-tuple-element.121) | data formatting | bytes 2359296 | tf_op jit(solution)/shard_map/while/body/eval_jaxpr/squeeze | solution.py:127
  160.6 2.3 %fusion.58 = bf16[192,3,128]{2,0,1:T(8,128)(2,1)S(1)} fusion(bf16[1536,3,128]{2,1,0:T(4,128)(2,1)} %reshape.315, f32[3,192,1536]{2,1,0:T(8,128)S(1)} %get-tuple-element.123, f32[3,192]{1,0:T(4,128)S(1)} %get-tuple-element.124, f32[192,3]{0,1:T(4,128)S(1)} %bitcast.84), kind=kOutput, calls=%fused_computation.12.clone.1 | convolution fusion | flops 228409344 | bytes 4870656 | tf_op jit(solution)/shard_map/while/body/eval_jaxpr/hqk,khd->qhd/dot_general | solution.py:82
  164.5 3.8 %gather_fusion = bf16[8,2,192,384]{3,2,1,0:T(8,128)(2,1)S(1)} fusion(bf16[2,21,192,384]{3,2,1,0:T(8,128)(2,1)} %get-tuple-element.140, s32[1024]{0:T(1024)S(1)} %pad_clamp_fusion.2), kind=kCustom, calls=%fused_computation.clone.1 | custom fusion | bytes 4718624 | tf_op jit(solution)/shard_map/while/body/eval_jaxpr/jit(_take)/gather | solution.py:126
  172.5 2.2 %fusion.56 = (f32[3,192]{1,0:T(4,128)S(1)}, f32[3,192,1536]{2,1,0:T(8,128)S(1)}) fusion(bf16[1536,3,128]{2,1,0:T(4,128)(2,1)} %reshape.316, bf16[3,192,3,128]{3,1,2,0:T(8,128)(2,1)} %get-tuple-element.141, s32[]{:T(128)} %get-tuple-element.131), kind=kOutput, calls=%fused_computation.87.clone.1 | convolution fusion | flops 228261312 | bytes 5262080 | tf_op jit(solution)/shard_map/while/body/eval_jaxpr/qhd,khd->hqk/dot_general | solution.py:75
  175.4 4.1 %reshape.315 = bf16[1536,3,128]{2,1,0:T(4,128)(2,1)} reshape(bf16[1,8,192,384]{3,2,0,1:T(8,128)(2,1)} %get-tuple-element.121) | data formatting | bytes 2359296 | tf_op jit(solution)/shard_map/while/body/eval_jaxpr/squeeze | solution.py:127
  179.4 2.3 %fusion.58 = bf16[192,3,128]{2,0,1:T(8,128)(2,1)S(1)} fusion(bf16[1536,3,128]{2,1,0:T(4,128)(2,1)} %reshape.315, f32[3,192,1536]{2,1,0:T(8,128)S(1)} %get-tuple-element.123, f32[3,192]{1,0:T(4,128)S(1)} %get-tuple-element.124, f32[192,3]{0,1:T(4,128)S(1)} %bitcast.84), kind=kOutput, calls=%fused_computation.12.clone.1 | convolution fusion | flops 228409344 | bytes 4870656 | tf_op jit(solution)/shard_map/while/body/eval_jaxpr/hqk,khd->qhd/dot_general | solution.py:82
  182.7 15.6 %all_to_all.67 = bf16[8,72,384]{2,1,0:T(8,128)(2,1)S(1)} all-to-all(bf16[8,72,384]{2,1,0:T(8,128)(2,1)} %bitcast.83), channel_id=1, replica_groups=mesh['blk'=64,'uly'=8] {'uly'}, dimensions={0} | all-to-all | bytes 884736 | tf_op jit(solution)/shard_map/all_to_all | solution.py:130
  (80 shorter events, 36.7 us)
Async XLA Ops:
  0.0 102.8 %copy-start = (s32[192,8]{0,1:T(8,128)S(1)}, s32[192,8]{0,1:T(8,128)}, u32[]{:S(2)}) copy-start(s32[192,8]{0,1:T(8,128)} %param.10) | copy-start | bytes 18436
  0.0 13.3 %copy-start.4 = (s32[192,3]{0,1:T(4,128)S(1)}, s32[192,3]{0,1:T(4,128)}, u32[]{:S(2)}) copy-start(s32[192,3]{0,1:T(4,128)} %param.11) | copy-start | bytes 6916
  1.8 25.6 %all-to-all-start = ((bf16[72,8,384]{2,0,1:T(8,128)(2,1)}), bf16[72,8,384]{2,0,1:T(8,128)(2,1)S(1)}, u32[]{:S(2)}, u32[]{:S(2)}) async-start(bf16[72,8,384]{2,0,1:T(8,128)(2,1)} %bitcast.59), calls=%async_computation | async-start | bytes 884736 | tf_op jit(solution)/shard_map/all_to_all | solution.py:90
  27.5 17.4 %all-to-all-start.2 = ((bf16[72,8,384]{2,0,1:T(8,128)(2,1)}), bf16[72,8,384]{2,0,1:T(8,128)(2,1)S(1)}, u32[]{:S(2)}, u32[]{:S(2)}) async-start(bf16[72,8,384]{2,0,1:T(8,128)(2,1)} %bitcast.57), calls=%async_computation.2 | async-start | bytes 884736 | tf_op jit(solution)/shard_map/all_to_all | solution.py:89
  44.9 17.2 %all-to-all-start.1 = ((bf16[72,8,384]{2,0,1:T(8,128)(2,1)}), bf16[72,8,384]{2,0,1:T(8,128)(2,1)S(1)}, u32[]{:S(2)}, u32[]{:S(2)}) async-start(bf16[72,8,384]{2,0,1:T(8,128)(2,1)} %bitcast.58), calls=%async_computation.1 | async-start | bytes 884736 | tf_op jit(solution)/shard_map/all_to_all | solution.py:91
  62.2 22.1 %collective-permute-start = (bf16[2,576,384]{2,1,0:T(8,128)(2,1)S(1)}, bf16[2,576,384]{2,1,0:T(8,128)(2,1)S(1)}, u32[]{:S(2)}, u32[]{:S(2)}) collective-permute-start(bf16[2,576,384]{2,1,0:T(8,128)(2,1)S(1)} %pad_maximum_fusion), channel_id=1, source_target_pairs={{0,8},{8,16},{16,24},{24,32},{32,40},{40,48},{48,56},{56,64},{64,7... | collective-permute-start | bytes 2654216 | tf_op jit(solution)/shard_map/ppermute | solution.py:21
  64.1 22.1 %collective-permute-start.3 = (bf16[2,576,384]{2,1,0:T(8,128)(2,1)S(1)}, bf16[2,576,384]{2,1,0:T(8,128)(2,1)S(1)}, u32[]{:S(2)}, u32[]{:S(2)}) collective-permute-start(bf16[2,576,384]{2,1,0:T(8,128)(2,1)S(1)} %pad_maximum_fusion), channel_id=1, source_target_pairs={{8,0},{16,8},{24,16},{32,24},{40,32},{48,40},{56,48},{64,56},{72,6... | collective-permute-start | bytes 2654216 | tf_op jit(solution)/shard_map/ppermute | solution.py:21
  84.3 1.9 copy-start.2
  84.3 16.6 %collective-permute-start.1 = (bf16[2,576,384]{2,1,0:T(8,128)(2,1)S(1)}, bf16[2,576,384]{2,1,0:T(8,128)(2,1)}, u32[]{:S(2)}, u32[]{:S(2)}) collective-permute-start(bf16[2,576,384]{2,1,0:T(8,128)(2,1)S(1)} %collective-permute-done), channel_id=1, source_target_pairs={{0,8},{8,16},{16,24},{24,32},{32,40},{40,48},{48,56},{56,64},{64,7... | collective-permute-start | bytes 2654216 | tf_op jit(solution)/shard_map/ppermute | solution.py:21
  86.2 17.3 %collective-permute-start.4 = (bf16[2,576,384]{2,1,0:T(8,128)(2,1)S(1)}, bf16[2,576,384]{2,1,0:T(8,128)(2,1)}, u32[]{:S(2)}, u32[]{:S(2)}) collective-permute-start(bf16[2,576,384]{2,1,0:T(8,128)(2,1)S(1)} %collective-permute-done.3), channel_id=1, source_target_pairs={{8,0},{16,8},{24,16},{32,24},{40,32},{48,40},{56,48},{64,56},{72,6... | collective-permute-start | bytes 2654216 | tf_op jit(solution)/shard_map/ppermute | solution.py:21
  100.9 16.8 %collective-permute-start.2 = (bf16[2,576,384]{2,1,0:T(8,128)(2,1)}, bf16[2,576,384]{2,1,0:T(8,128)(2,1)}, u32[]{:S(2)}, u32[]{:S(2)}) collective-permute-start(bf16[2,576,384]{2,1,0:T(8,128)(2,1)} %collective-permute-done.1), channel_id=1, source_target_pairs={{0,8},{8,16},{16,24},{24,32},{32,40},{40,48},{48,56},{56,64},{64,7... | collective-permute-start | bytes 2654216 | tf_op jit(solution)/shard_map/ppermute | solution.py:21
  103.6 18.6 %collective-permute-start.5 = (bf16[2,576,384]{2,1,0:T(8,128)(2,1)}, bf16[2,576,384]{2,1,0:T(8,128)(2,1)}, u32[]{:S(2)}, u32[]{:S(2)}) collective-permute-start(bf16[2,576,384]{2,1,0:T(8,128)(2,1)} %collective-permute-done.4), channel_id=1, source_target_pairs={{8,0},{16,8},{24,16},{32,24},{40,32},{48,40},{56,48},{64,56},{72,6... | collective-permute-start | bytes 2654216 | tf_op jit(solution)/shard_map/ppermute | solution.py:21
  110.4 9.8 %copy-start.3 = (bf16[2,576,384]{2,1,0:T(8,128)(2,1)S(1)}, bf16[2,576,384]{2,1,0:T(8,128)(2,1)}, u32[]{:S(2)}) copy-start(bf16[2,576,384]{2,1,0:T(8,128)(2,1)} %copy-done.2) | copy-start | bytes 2654212
  123.5 2.6 %copy-start.1 = (bf16[2,4032,384]{2,1,0:T(8,128)(2,1)}, bf16[2,4032,384]{2,1,0:T(8,128)(2,1)S(1)}, u32[]{:S(2)}) copy-start(bf16[2,4032,384]{2,1,0:T(8,128)(2,1)S(1)} %constant_dynamic-update-slice_fusion.1) | copy-start | bytes 18579460
where the time goes:
time: 201 us; the launch traced here: 199 us
  waiting for transfers between devices  59.6 us (30%)
  local copies, waits for them, and re-layouts  55.7 us (28%)
  starting transfers between devices  43.3 us (22%)
  blocking collectives  15.6 us (8%)
  matrix products  13.5 us (7%)
  other arithmetic  11 us (5%)
    ppermute x6, starting transfers between devices, shifted(): lax.ppermute(value, axis, [(source, source + steps) for source in range(l...  28.6 us
    ppermute x6, waiting for transfers between devices, shifted(): lax.ppermute(value, axis, [(source, source + steps) for source in range(l...  24.9 us
    squeeze x6, local copies, waits for them, and re-layouts, one_tile(): return attend(query_tile, picked[0], picked[1])  17.7 us
    all_to_all x1, blocking collectives, on_device(): lax.all_to_all(attended.reshape(row_count, columns), 'uly', split_axis=0,...  15.6 us
    all_to_all x1, waiting for transfers between devices, on_device(): lax.all_to_all(keys, 'uly', split_axis=1, concat_axis=0, tiled=True)  14.1 us
    all_to_all x1, waiting for transfers between devices, on_device(): lax.all_to_all(queries, 'uly', split_axis=1, concat_axis=0, tiled=True)  12.1 us
    gather x3, local copies, waits for them, and re-layouts, one_tile(): jnp.take(window, chosen, axis=1)  11.5 us
    all_to_all x1, waiting for transfers between devices, on_device(): lax.all_to_all(values, 'uly', split_axis=1, concat_axis=0, tiled=True)  8.49 us
  transfers between devices with their start and end apart: 9, of which 6 were waited for; matrix products, arithmetic and copies ran while one was open for 9% of the time, Pallas kernels for 0%

commit v1 on v0

v1 whole, which is shorter than its diff:
```python
import functools
import math

import jax
import jax.numpy as jnp
from jax import lax
from jax.experimental import pallas as pl
from jax.experimental.pallas import tpu as pltpu
from jax.sharding import PartitionSpec as P

HEAD_DIM = 128
TF = 3
TH = 8
TW = 8
GF = 2
GH = 3
KPT = 8
TILE = 192
MESH = pl.DeviceIdType.MESH


def rope_tables(tile_coords, first_token, count):
    token = first_token + jnp.arange(count, dtype=jnp.int32)
    offset = token % TILE
    first_tile = first_token // TILE
    near = lax.dynamic_slice_in_dim(tile_coords, first_tile, 1, 0)
    far = lax.dynamic_slice_in_dim(tile_coords, (first_token + count - 1) // TILE, 1, 0)
    coords = jnp.where((token // TILE == first_tile)[:, None], near, far)
    frame_pos = (coords[:, 0] * TF + offset // (TH * TW)).astype(jnp.float32)
    height_pos = (coords[:, 1] * TH + offset // TW % TH).astype(jnp.float32)
    width_pos = (coords[:, 2] * TW + offset % TW).astype(jnp.float32)
    halves = HEAD_DIM // 2
    side_pairs = HEAD_DIM // 6
    frame_pairs = halves - 2 * side_pairs
    lane = jnp.arange(HEAD_DIM, dtype=jnp.int32)
    pair = lane % halves
    in_frame = pair < frame_pairs
    in_height = pair < frame_pairs + side_pairs
    within = jnp.where(
        in_frame, pair, jnp.where(in_height, pair - frame_pairs, pair - frame_pairs - side_pairs)
    ).astype(jnp.float32)
    axis_len = jnp.where(in_frame, frame_pairs, side_pairs).astype(jnp.float32)
    frequency = jnp.exp(-math.log(10000.0) * within / axis_len)
    position = jnp.where(
        in_frame, frame_pos[:, None], jnp.where(in_height, height_pos[:, None], width_pos[:, None])
    )
    angles = position * frequency
    sign = jnp.where(lane < halves, -1.0, 1.0)
    return jnp.cos(angles), jnp.sin(angles) * sign


def kernel(
    uly, heads_here, cols,
    sel_ref, cos_ref, sin_ref, q_ref, k_ref, v_ref,
    out_ref,
    kv_stage, q_stage, kv_in, q_in, win0, win1, win2, q_rows, o_rows, o_stage,
    kv_ssem, kv_rsem, q_ssem, q_rsem, z_ssem, z_rsem, f_ssem, f_rsem, o_ssem, o_rsem,
):
    wins = (win0, win1, win2)
    heads = uly * heads_here
    chunk = q_ref.shape[0]
    run = chunk * uly
    blk = lax.axis_index("blk")
    me = lax.axis_index("uly")
    core = lax.rem(blk, 2)
    col = lax.div(blk, 2)
    has_left = col > 0
    has_right = col < cols - 1
    peers = [lax.rem(me + step, uly) for step in (1, 3, 5, 7, 2, 6, 4)]
    other = blk + 1 - 2 * core

    barrier = pltpu.get_barrier_semaphore()
    for peer in peers:
        pl.semaphore_signal(barrier, inc=1, device_id=(blk, peer), device_id_type=MESH)
    pl.semaphore_signal(barrier, inc=1, device_id=(other, me), device_id_type=MESH)

    @pl.when(has_left)
    def _():
        pl.semaphore_signal(barrier, inc=1, device_id=(blk - 2, me), device_id_type=MESH)

    @pl.when(has_right)
    def _():
        pl.semaphore_signal(barrier, inc=1, device_id=(blk + 2, me), device_id_type=MESH)

    cosine = cos_ref[...]
    sine = sin_ref[...]

    def rotated(rows):
        rows = rows.astype(jnp.float32)
        return (rows * cosine + pltpu.roll(rows, HEAD_DIM // 2, 1) * sine).astype(jnp.bfloat16)

    def stage_kv(head, carry):
        lanes = pl.ds(pl.multiple_of(head * HEAD_DIM, HEAD_DIM), HEAD_DIM)
        kv_stage[head, 0] = rotated(k_ref[:, lanes])
        kv_stage[head, 1] = v_ref[:, lanes]
        return carry

    def stage_q(head, carry):
        lanes = pl.ds(pl.multiple_of(head * HEAD_DIM, HEAD_DIM), HEAD_DIM)
        q_stage[head] = rotated(q_ref[:, lanes])
        return carry

    lax.fori_loop(0, heads, stage_kv, 0)
    pl.semaphore_wait(barrier, uly + has_left.astype(jnp.int32) + has_right.astype(jnp.int32))

    def exchange(stage, landing, ssem, rsem, j):
        for peer in peers:
            pltpu.make_async_remote_copy(
                src_ref=stage.at[peer * heads_here + j],
                dst_ref=landing.at[j, me],
                send_sem=ssem.at[j],
                recv_sem=rsem.at[j],
                device_id=(blk, peer),
                device_id_type=MESH,
            ).start()
        pltpu.make_async_copy(
            stage.at[me * heads_here + j], landing.at[j, me], rsem.at[j]
        ).start()

    for j in range(heads_here):
        exchange(kv_stage, kv_in, kv_ssem, kv_rsem, j)
    lax.fori_loop(0, heads, stage_q, 0)
    for j in range(heads_here):
        exchange(q_stage, q_in, q_ssem, q_rsem, j)

    tiles = run // TILE
    mine = pl.ds(core * tiles, tiles)
    theirs = pl.ds((1 - core) * tiles, tiles)

    def to_other(j, slot):
        rows = wins[j].at[slot, mine]
        return pltpu.make_async_remote_copy(
            src_ref=rows, dst_ref=rows, send_sem=f_ssem.at[j, slot], recv_sem=f_rsem.at[j, slot],
            device_id=(other, me), device_id_type=MESH,
        )

    def from_other(j, slot):
        rows = wins[j].at[slot, theirs]
        return pltpu.make_async_copy(rows, rows, f_rsem.at[j, slot])

    def to_left(j):
        return pltpu.make_async_remote_copy(
            src_ref=wins[j].at[1, mine], dst_ref=wins[j].at[2, mine],
            send_sem=z_ssem.at[j, 0], recv_sem=z_rsem.at[j, 0],
            device_id=(blk - 2, me), device_id_type=MESH,
        )

    def to_right(j):
        return pltpu.make_async_remote_copy(
            src_ref=wins[j].at[1, mine], dst_ref=wins[j].at[0, mine],
            send_sem=z_ssem.at[j, 1], recv_sem=z_rsem.at[j, 1],
            device_id=(blk + 2, me), device_id_type=MESH,
        )

    def gather_rows(landing, index, store):
        for pair in range(uly // 2):
            both = jnp.concatenate(
                [landing[index(2 * pair)].astype(jnp.float32), landing[index(2 * pair + 1)].astype(jnp.float32)],
                axis=0,
            ).astype(jnp.bfloat16)
            first, past = 2 * chunk * pair, 2 * chunk * (pair + 1)
            for tile in range(first // TILE, (past - 1) // TILE + 1):
                start, stop = max(first, tile * TILE), min(past, (tile + 1) * TILE)
                store(tile, start - tile * TILE, both[start - first : stop - first])

    def spread(j):
        pltpu.make_async_copy(kv_in.at[j], kv_in.at[j], kv_rsem.at[j]).wait()
        for which in range(2):
            def store(tile, row, value):
                wins[j][1, core * tiles + tile, which, pl.ds(row, value.shape[0])] = value
            gather_rows(kv_in, lambda s: (j, s, which), store)

        @pl.when(has_right)
        def _():
            to_right(j).start()

        @pl.when(has_left)
        def _():
            to_left(j).start()

        to_other(j, 1).start()

    def forward(j):
        @pl.when(has_left)
        def _():
            rows = wins[j].at[0, mine]
            pltpu.make_async_copy(rows, rows, z_rsem.at[j, 1]).wait()
            to_other(j, 0).start()

        @pl.when(has_right)
        def _():
            rows = wins[j].at[2, mine]
            pltpu.make_async_copy(rows, rows, z_rsem.at[j, 0]).wait()
            to_other(j, 2).start()

    factor = HEAD_DIM ** -0.5 * math.log2(math.e)
    listed = KPT // 2

    def attend(j):
        pltpu.make_async_copy(q_in.at[j], q_in.at[j], q_rsem.at[j]).wait()
        def store(tile, row, value):
            q_rows[tile, pl.ds(row, value.shape[0])] = value
        gather_rows(q_in, lambda s: (j, s), store)
        from_other(j, 1).wait()

        @pl.when(has_left)
        def _():
            from_other(j, 0).wait()

        @pl.when(has_right)
        def _():
            from_other(j, 2).wait()

        def one_tile(tile, carry):
            side = sel_ref[tile, 0]
            first = sel_ref[tile, 1]

            def rows_of(slot, which):
                return jnp.concatenate(
                    [wins[j][slot, first + step, which] for step in range(listed)], axis=0
                )

            rows = pl.ds(pl.multiple_of(tile * TILE, TILE), TILE)
            query = q_rows[tile]
            contract = (((1,), (1,)), ((), ()))
            near = lax.dot_general(
                query, rows_of(1, 0), contract, preferred_element_type=jnp.float32
            )
            far = lax.dot_general(
                query, rows_of(side, 0), contract, preferred_element_type=jnp.float32
            )
            largest = jnp.maximum(
                jnp.max(near, axis=1, keepdims=True), jnp.max(far, axis=1, keepdims=True)
            )
            near = jnp.exp2((near - largest) * factor)
            far = jnp.exp2((far - largest) * factor)
            total = jnp.sum(near, axis=1, keepdims=True) + jnp.sum(far, axis=1, keepdims=True)
            summed = jnp.dot(
                near.astype(jnp.bfloat16), rows_of(1, 1), preferred_element_type=jnp.float32
            ) + jnp.dot(
                far.astype(jnp.bfloat16), rows_of(side, 1), preferred_element_type=jnp.float32
            )
            o_rows[rows] = summed / total
            return carry

        lax.fori_loop(0, tiles, one_tile, 0)
        for part in range(uly):
            o_stage[j, part] = o_rows[pl.ds(part * chunk, chunk)].astype(jnp.bfloat16)
        lanes = pl.ds(pl.multiple_of((me * heads_here + j) * HEAD_DIM, HEAD_DIM), HEAD_DIM)
        for peer in peers:
            pltpu.make_async_remote_copy(
                src_ref=o_stage.at[j, peer],
                dst_ref=out_ref.at[:, lanes],
                send_sem=o_ssem.at[j],
                recv_sem=o_rsem,
                device_id=(blk, peer),
                device_id_type=MESH,
            ).start()
        pltpu.make_async_copy(o_stage.at[j, me], out_ref.at[:, lanes], o_rsem).start()

    spread(0)
    spread(1)
    forward(0)
    spread(2)
    forward(1)
    attend(0)
    forward(2)
    attend(1)
    attend(2)

    sent = pl.ds(0, uly - 1)
    for j in range(heads_here):
        pltpu.make_async_copy(kv_in.at[j, sent], kv_in.at[j, sent], kv_ssem.at[j]).wait()
        pltpu.make_async_copy(q_in.at[j, sent], q_in.at[j, sent], q_ssem.at[j]).wait()
        to_other(j, 1).wait_send()

        @pl.when(has_left)
        def _():
            to_left(j).wait_send()
            to_other(j, 0).wait_send()

        @pl.when(has_right)
        def _():
            to_right(j).wait_send()
            to_other(j, 2).wait_send()

        pltpu.make_async_copy(o_stage.at[j, sent], o_stage.at[j, sent], o_ssem.at[j]).wait()
    pltpu.make_async_copy(out_ref, out_ref, o_rsem).wait()


def on_device(cols, queries, keys, values, tile_pairs, tile_coords):
    uly = lax.axis_size("uly")
    chunk, columns = queries.shape
    heads_here = columns // HEAD_DIM // uly
    run = chunk * uly
    tiles = run // TILE
    blk = lax.axis_index("blk")
    first_token = blk * run + lax.axis_index("uly") * chunk
    cosine, sine = rope_tables(tile_coords, first_token, chunk)
    lowest = jnp.min(lax.dynamic_slice_in_dim(tile_pairs, blk * tiles, tiles, 0), axis=1)
    side = 2 * (lowest // (GF * GH) - blk // 2 + 1)
    first = lowest % (GF * GH)
    sel = jnp.stack((side, first), axis=1)
    vmem = pl.BlockSpec(memory_space=pltpu.VMEM)
    dma = pltpu.SemaphoreType.DMA
    bf16 = jnp.bfloat16
    heads = uly * heads_here
    window = pltpu.VMEM((3, 2 * tiles, 2, TILE, HEAD_DIM), bf16)
    return pl.pallas_call(
        functools.partial(kernel, uly, heads_here, cols),
        out_shape=jax.ShapeDtypeStruct(queries.shape, bf16),
        in_specs=[pl.BlockSpec(memory_space=pltpu.SMEM)] + [vmem] * 5,
        out_specs=vmem,
        scratch_shapes=[
            pltpu.VMEM((heads, 2, chunk, HEAD_DIM), bf16),
            pltpu.VMEM((heads, chunk, HEAD_DIM), bf16),
            pltpu.VMEM((heads_here, uly, 2, chunk, HEAD_DIM), bf16),
            pltpu.VMEM((heads_here, uly, chunk, HEAD_DIM), bf16),
            window, window, window,
            pltpu.VMEM((tiles, TILE, HEAD_DIM), bf16),
            pltpu.VMEM((run, HEAD_DIM), jnp.float32),
            pltpu.VMEM((heads_here, uly, chunk, HEAD_DIM), bf16),
            dma((heads_here,)), dma((heads_here,)),
            dma((heads_here,)), dma((heads_here,)),
            dma((heads_here, 2)), dma((heads_here, 2)),
            dma((heads_here, 3)), dma((heads_here, 3)),
            dma((heads_here,)), dma(()),
        ],
        compiler_params=pltpu.CompilerParams(
            collective_id=0, has_side_effects=True, vmem_limit_bytes=40 * 2 ** 20
        ),
    )(sel, cosine, sine, queries, keys, values)


def solution(mesh):
    spec = P(("blk", "uly"), None)
    return jax.shard_map(
        functools.partial(on_device, mesh.shape["blk"] // 2),
        mesh=mesh,
        in_specs=(spec, spec, spec, P(), P()),
        out_specs=spec,
        check_vma=False,
    )
```

time: 201 us -> 83.9 us (0.42)
  the two profiles are of different devices: /device:TPU:16 before, /device:TPU:46 now
where the time goes in v1:
time: 83.9 us; the launch traced here: 83.7 us
  Pallas kernels  78 us (93%)
  local copies, waits for them, and re-layouts  4.99 us (6%)
    pallas_call x1, Pallas kernels, on_device(): pl.pallas_call(functools.partial(kernel, uly, heads_here, cols), out_shap...  78 us
    unnamed x11, local copies, waits for them, and re-layouts  4.48 us

profile of v1, /device:TPU:46, one launch (start us, length us, event | category | flops | bytes accessed | tf_op | source)
XLA Modules:
  0.0 83.7 jit_solution(15583607879502796426)
XLA Ops:
  0.0 0.0 copy-start
  0.0 0.0 copy-start.4
  0.0 0.7 copy-done
  0.7 0.1 dynamic-slice_reduce_fusion
  0.8 0.0 copy-done.4
  0.8 0.2 dynamic-slice_reduce_fusion.2
  1.0 0.1 broadcast_select_fusion
  1.1 0.1 copy.7
  1.3 0.1 copy.8
  1.4 0.1 copy.6
  1.5 0.1 pad_add_fusion.sel_ref
  1.6 0.2 sine_multiply_fusion
  1.8 0.0 copy-start.1
  1.8 1.0 %copy-done.1 = bf16[72,3072]{1,0:T(8,128)(2,1)S(1)} copy-done((bf16[72,3072]{1,0:T(8,128)(2,1)S(1)}, bf16[72,3072]{1,0:T(8,128)(2,1)}, u32[]{:S(2)}) %copy-start.1) | copy-done | bytes 442392
  2.8 0.0 copy-start.2
  2.8 1.0 %copy-done.2 = bf16[72,3072]{1,0:T(8,128)(2,1)S(1)} copy-done((bf16[72,3072]{1,0:T(8,128)(2,1)S(1)}, bf16[72,3072]{1,0:T(8,128)(2,1)}, u32[]{:S(2)}) %copy-start.2) | copy-done | bytes 442392
  3.8 0.0 copy-start.3
  3.8 1.0 %copy-done.3 = bf16[72,3072]{1,0:T(8,128)(2,1)S(1)} copy-done((bf16[72,3072]{1,0:T(8,128)(2,1)S(1)}, bf16[72,3072]{1,0:T(8,128)(2,1)}, u32[]{:S(2)}) %copy-start.3) | copy-done | bytes 442392
  4.8 78.0 %shard_map.55 = bf16[72,3072]{1,0:T(8,128)(2,1)S(1)} custom-call(s32[3,2]{1,0:T(4,128)S(1)} %pad_add_fusion.sel_ref, f32[72,128]{1,0:T(8,128)S(1)} %get-tuple-element.8.cos_ref, f32[72,128]{1,0:T(8,128)S(1)} %get-tuple-element.7.sin_ref, bf16[72,3072]{1,0:T(8,128)(2,1)S(1)} %copy-done.1, bf16[72,3072]{1,0:T(8,128)(2,1)S(1)} %copy-done.2, ...), custom_call_target="tpu_custom_call" | custom-call | tf_op jit(solution)/shard_map/pallas_call | solution.py:309
  82.9 0.8 copy.14
  (7 shorter events, 0.1 us)
Async XLA Ops:
  0.0 0.7 copy-start
  0.0 0.8 copy-start.4
  1.8 1.0 %copy-start.1 = (bf16[72,3072]{1,0:T(8,128)(2,1)S(1)}, bf16[72,3072]{1,0:T(8,128)(2,1)}, u32[]{:S(2)}) copy-start(bf16[72,3072]{1,0:T(8,128)(2,1)} %q_ref.1) | copy-start | bytes 1327108
  2.8 1.0 %copy-start.2 = (bf16[72,3072]{1,0:T(8,128)(2,1)S(1)}, bf16[72,3072]{1,0:T(8,128)(2,1)}, u32[]{:S(2)}) copy-start(bf16[72,3072]{1,0:T(8,128)(2,1)} %k_ref.1) | copy-start | bytes 1327108
  3.8 1.0 %copy-start.3 = (bf16[72,3072]{1,0:T(8,128)(2,1)S(1)}, bf16[72,3072]{1,0:T(8,128)(2,1)}, u32[]{:S(2)}) copy-start(bf16[72,3072]{1,0:T(8,128)(2,1)} %v_ref.1) | copy-start | bytes 1327108

commit v2 on v1

v2 whole, which is shorter than its diff:
```python
import functools
import math

import jax
import jax.numpy as jnp
from jax import lax
from jax.experimental import pallas as pl
from jax.experimental.pallas import tpu as pltpu
from jax.sharding import PartitionSpec as P

HEAD_DIM = 128
TF = 3
TH = 8
TW = 8
GF = 2
GH = 3
KPT = 8
TILE = 192
LINE = 8
MESH = pl.DeviceIdType.MESH


def rope_tables(coords, row, offset, count):
    shape = (count, HEAD_DIM)
    token = lax.broadcasted_iota(jnp.int32, shape, 0) + offset
    lane = lax.broadcasted_iota(jnp.int32, shape, 1)
    past = token >= TILE
    token = jnp.where(past, token - TILE, token)
    last = row + lax.div(offset + count - 1, TILE)

    def cell(axis):
        return jnp.where(past, coords[last, axis], coords[row, axis])

    halves = HEAD_DIM // 2
    side_pairs = HEAD_DIM // 6
    frame_pairs = halves - 2 * side_pairs
    pair = jnp.where(lane < halves, lane, lane - halves)
    in_frame = pair < frame_pairs
    in_height = pair < frame_pairs + side_pairs
    within = jnp.where(
        in_frame, pair, jnp.where(in_height, pair - frame_pairs, pair - frame_pairs - side_pairs)
    ).astype(jnp.float32)
    axis_len = jnp.where(in_frame, float(frame_pairs), float(side_pairs))
    frequency = jnp.exp(-math.log(10000.0) * within / axis_len)
    position = jnp.where(
        in_frame,
        cell(0) * TF + lax.div(token, TH * TW),
        jnp.where(
            in_height,
            cell(1) * TH + lax.rem(lax.div(token, TW), TH),
            cell(2) * TW + lax.rem(token, TW),
        ),
    ).astype(jnp.float32)
    angles = position * frequency
    return jnp.cos(angles), jnp.where(lane < halves, -jnp.sin(angles), jnp.sin(angles))


def kernel(
    uly, heads_here, cols, line,
    q_hbm, k_hbm, v_hbm, pairs_hbm, coords_hbm,
    out_ref,
    kv_stage, q_stage, kv_in, q_in, win0, win1, win2, q_rows, o_rows, o_stage,
    kv_ssem, kv_rsem, q_ssem, q_rsem, z_ssem, z_rsem, f_ssem, f_rsem, o_ssem, o_rsem,
    relay_buf, r_ssem, r_rsem, q_ref, k_ref, v_ref, pairs, coords, in_sem,
):
    wins = (win0, win1, win2)
    heads = uly * heads_here
    chunk = q_ref.shape[0]
    run = chunk * uly
    blk = lax.axis_index("blk")
    me = lax.axis_index("uly")
    tiles = run // TILE
    some = pairs.shape[0]
    window_row = jnp.minimum(lax.div(blk * tiles, 8) * 8, pairs_hbm.shape[0] - some)
    near_rows = pl.ds(pl.multiple_of(window_row, 8), some)
    loads = [
        pltpu.make_async_copy(src, dst, in_sem.at[n])
        for n, (src, dst) in enumerate((
            (coords_hbm.at[near_rows], coords),
            (k_hbm, k_ref),
            (v_hbm, v_ref),
            (q_hbm, q_ref),
            (pairs_hbm.at[near_rows], pairs),
        ))
    ]
    for load in loads:
        load.start()
    core = lax.rem(blk, 2)
    col = lax.div(blk, 2)
    has_left = col > 0
    has_right = col < cols - 1
    place = lax.rem(col, line)
    cross_left = (place == 0) & has_left
    cross_right = (place == line - 1) & has_right
    bend_right = (place == 0) & (col < cols - line)
    bend_left = (place == line - 1) & (col >= line)
    skip_right = (place == line - 2) & (col < cols - line)
    skip_left = (place == 1) & (col >= line)
    row = 2 * line
    peers = [lax.rem(me + step, uly) for step in (1, 3, 5, 7, 2, 6, 4)]
    other = blk + 1 - 2 * core

    barrier = pltpu.get_barrier_semaphore()
    for peer in peers:
        pl.semaphore_signal(barrier, inc=1, device_id=(blk, peer), device_id_type=MESH)
    pl.semaphore_signal(barrier, inc=1, device_id=(other, me), device_id_type=MESH)

    @pl.when(has_left)
    def _():
        pl.semaphore_signal(barrier, inc=1, device_id=(blk - 2, me), device_id_type=MESH)

    @pl.when(has_right)
    def _():
        pl.semaphore_signal(barrier, inc=1, device_id=(blk + 2, me), device_id_type=MESH)

    extra = (
        (cross_left, blk - row),
        (cross_left, blk + row - 2),
        (cross_left, blk - 4),
        (cross_right, blk + row),
        (cross_right, blk - row + 2),
        (cross_right, blk + 4),
        (bend_right, blk + row - 2),
        (bend_right, blk + row),
        (bend_left, blk - row + 2),
        (bend_left, blk - row),
        (skip_right, blk + 4),
        (skip_left, blk - 4),
    )
    greeted = uly
    for due, target in ((has_left, None), (has_right, None)) + extra:
        greeted = greeted + due.astype(jnp.int32)
    for due, target in extra:

        @pl.when(due)
        def _():
            pl.semaphore_signal(barrier, inc=1, device_id=(target, me), device_id_type=MESH)

    loads[0].wait()
    cosine, sine = rope_tables(
        coords,
        blk * tiles + lax.div(me * chunk, TILE) - window_row,
        lax.rem(me * chunk, TILE),
        chunk,
    )

    def rotated(rows):
        rows = rows.astype(jnp.float32)
        return (rows * cosine + pltpu.roll(rows, HEAD_DIM // 2, 1) * sine).astype(jnp.bfloat16)

    def stage_kv(j, peer, carry):
        head = peer * heads_here + j
        lanes = pl.ds(pl.multiple_of(head * HEAD_DIM, HEAD_DIM), HEAD_DIM)
        kv_stage[head, 0] = rotated(k_ref[:, lanes])
        kv_stage[head, 1] = v_ref[:, lanes]
        return carry

    def stage_q(j, peer, carry):
        head = peer * heads_here + j
        lanes = pl.ds(pl.multiple_of(head * HEAD_DIM, HEAD_DIM), HEAD_DIM)
        q_stage[head] = rotated(q_ref[:, lanes])
        return carry

    loads[1].wait()
    loads[2].wait()
    lax.fori_loop(0, uly, functools.partial(stage_kv, 0), 0)
    pl.semaphore_wait(barrier, greeted)

    def exchange(stage, landing, ssem, rsem, j):
        for peer in peers:
            pltpu.make_async_remote_copy(
                src_ref=stage.at[peer * heads_here + j],
                dst_ref=landing.at[j, me],
                send_sem=ssem.at[j],
                recv_sem=rsem.at[j],
                device_id=(blk, peer),
                device_id_type=MESH,
            ).start()
        pltpu.make_async_copy(
            stage.at[me * heads_here + j], landing.at[j, me], rsem.at[j]
        ).start()

    for j in range(heads_here):
        if j:
            lax.fori_loop(0, uly, functools.partial(stage_kv, j), 0)
        exchange(kv_stage, kv_in, kv_ssem, kv_rsem, j)
    loads[3].wait()
    for j in range(heads_here):
        lax.fori_loop(0, uly, functools.partial(stage_q, j), 0)
    loads[4].wait()

    choice = []
    for tile in range(tiles):
        row_here = blk * tiles + tile - window_row
        lowest = pairs[row_here, 0]
        for slot in range(1, KPT):
            lowest = jnp.minimum(lowest, pairs[row_here, slot])
        across = lax.div(lowest, GF * GH)
        choice.append((
            jnp.where(across < col, 0, 2),
            jnp.clip(lowest - across * (GF * GH), 0, GF * GH - KPT // 2),
        ))

    mine = pl.ds(core * tiles, tiles)
    theirs = pl.ds((1 - core) * tiles, tiles)

    def to_other(j, slot):
        rows = wins[j].at[slot, mine]
        return pltpu.make_async_remote_copy(
            src_ref=rows, dst_ref=rows, send_sem=f_ssem.at[j, slot], recv_sem=f_rsem.at[j, slot],
            device_id=(other, me), device_id_type=MESH,
        )

    def from_other(j, slot):
        rows = wins[j].at[slot, theirs]
        return pltpu.make_async_copy(rows, rows, f_rsem.at[j, slot])

    def hop(src, dst, ssem, rsem, target):
        return pltpu.make_async_remote_copy(
            src_ref=src, dst_ref=dst, send_sem=ssem, recv_sem=rsem,
            device_id=(target, me), device_id_type=MESH,
        )

    last = tiles - 1

    def part(n):
        return core * tiles + last if n == 0 else pl.ds(core * tiles, last)

    def to_side(j, slot, target, n):
        return hop(
            wins[j].at[1, part(n)], wins[j].at[2 - slot, part(n)],
            z_ssem.at[j, slot // 2, n], z_rsem.at[j, 1 - slot // 2, n], target,
        )

    def direct(j, slot, target):
        return hop(
            wins[j].at[1, core * tiles], wins[j].at[2 - slot, core * tiles],
            z_ssem.at[j, slot // 2, 0], z_rsem.at[j, 1 - slot // 2, 0], target,
        )

    def bend_in(j, target):
        return hop(
            wins[j].at[1, core * tiles + 1], relay_buf.at[j],
            r_ssem.at[j, 0], r_rsem.at[j], target,
        )

    def bend_out(j, slot, target):
        return hop(
            relay_buf.at[j], wins[j].at[slot, core * tiles + 1],
            r_ssem.at[j, 1], z_rsem.at[j, slot // 2, 1], target,
        )

    def skip_out(j, slot, target):
        return hop(
            wins[j].at[slot, core * tiles + last], wins[j].at[2 - slot, core * tiles + last],
            r_ssem.at[j, 1], z_rsem.at[j, 1 - slot // 2, 2], target,
        )

    inner_right = has_right & ~cross_right
    inner_left = has_left & ~cross_left

    def sides(j):
        return (
            (cross_right, bend_in(j, blk - row + 2)),
            (cross_left, bend_in(j, blk + row - 2)),
            (inner_right, to_side(j, 2, blk + 2, 0)),
            (inner_left, to_side(j, 0, blk - 2, 0)),
            (cross_right, direct(j, 2, blk + 2)),
            (cross_left, direct(j, 0, blk - 2)),
            (inner_right, to_side(j, 2, blk + 2, 1)),
            (inner_left, to_side(j, 0, blk - 2, 1)),
        )

    def relays(j):
        return (
            (bend_right, bend_out(j, 0, blk + row)),
            (bend_left, bend_out(j, 2, blk - row)),
            (skip_right, skip_out(j, 2, blk + 4)),
            (skip_left, skip_out(j, 0, blk - 4)),
        )

    def start_all(copies):
        for due, copy in copies:

            @pl.when(due)
            def _():
                copy.start()

    def sent_all(copies):
        for due, copy in copies:

            @pl.when(due)
            def _():
                copy.wait_send()

    def arrived(rows, sem):
        pltpu.make_async_copy(rows, rows, sem).wait()

    def gather_rows(landing, index, store):
        for pair in range(uly // 2):
            both = jnp.concatenate(
                [landing[index(2 * pair)].astype(jnp.float32), landing[index(2 * pair + 1)].astype(jnp.float32)],
                axis=0,
            ).astype(jnp.bfloat16)
            first, past = 2 * chunk * pair, 2 * chunk * (pair + 1)
            for tile in range(first // TILE, (past - 1) // TILE + 1):
                start, stop = max(first, tile * TILE), min(past, (tile + 1) * TILE)
                store(tile, start - tile * TILE, both[start - first : stop - first])

    def spread(j):
        pltpu.make_async_copy(kv_in.at[j], kv_in.at[j], kv_rsem.at[j]).wait()
        for which in range(2):
            def store(tile, row, value):
                wins[j][1, core * tiles + tile, which, pl.ds(row, value.shape[0])] = value
            gather_rows(kv_in, lambda s: (j, s, which), store)

        start_all(sides(j))
        to_other(j, 1).start()

    def relay(j):
        @pl.when(bend_left | bend_right)
        def _():
            arrived(relay_buf.at[j], r_rsem.at[j])

        for slot, due in ((0, skip_left), (2, skip_right)):

            @pl.when(due)
            def _():
                arrived(wins[j].at[slot, part(0)], z_rsem.at[j, slot // 2, 0])

        start_all(relays(j))

    def forward(j):
        for slot, inner, skips, cross in (
            (0, inner_left, skip_left, cross_left),
            (2, inner_right, skip_right, cross_right),
        ):

            @pl.when(inner)
            def _():
                @pl.when(~skips)
                def _():
                    arrived(wins[j].at[slot, part(0)], z_rsem.at[j, slot // 2, 0])

                arrived(wins[j].at[slot, part(1)], z_rsem.at[j, slot // 2, 1])
                to_other(j, slot).start()

            @pl.when(cross)
            def _():
                for n in range(tiles):
                    arrived(wins[j].at[slot, core * tiles + n], z_rsem.at[j, slot // 2, n])
                to_other(j, slot).start()

    factor = HEAD_DIM ** -0.5 * math.log2(math.e)
    listed = KPT // 2

    def attend(j):
        pltpu.make_async_copy(q_in.at[j], q_in.at[j], q_rsem.at[j]).wait()
        def store(tile, row, value):
            q_rows[tile, pl.ds(row, value.shape[0])] = value
        gather_rows(q_in, lambda s: (j, s), store)
        from_other(j, 1).wait()

        @pl.when(has_left)
        def _():
            from_other(j, 0).wait()

        @pl.when(has_right)
        def _():
            from_other(j, 2).wait()

        lanes = pl.ds(pl.multiple_of((me * heads_here + j) * HEAD_DIM, HEAD_DIM), HEAD_DIM)
        for tile in range(tiles):
            side, first = choice[tile]

            def rows_of(slot, which):
                return jnp.concatenate(
                    [wins[j][slot, first + step, which] for step in range(listed)], axis=0
                )

            query = q_rows[tile]
            contract = (((1,), (1,)), ((), ()))
            near = lax.dot_general(
                query, rows_of(1, 0), contract, preferred_element_type=jnp.float32
            )
            far = lax.dot_general(
                query, rows_of(side, 0), contract, preferred_element_type=jnp.float32
            )
            largest = jnp.maximum(
                jnp.max(near, axis=1, keepdims=True), jnp.max(far, axis=1, keepdims=True)
            )
            near = jnp.exp2((near - largest) * factor)
            far = jnp.exp2((far - largest) * factor)
            total = jnp.sum(near, axis=1, keepdims=True) + jnp.sum(far, axis=1, keepdims=True)
            summed = jnp.dot(
                near.astype(jnp.bfloat16), rows_of(1, 1), preferred_element_type=jnp.float32
            ) + jnp.dot(
                far.astype(jnp.bfloat16), rows_of(side, 1), preferred_element_type=jnp.float32
            )
            o_rows[pl.ds(tile * TILE, TILE)] = summed / total
            for part_ in range(tile * TILE // chunk, (tile + 1) * TILE // chunk):
                o_stage[j, part_] = o_rows[pl.ds(part_ * chunk, chunk)].astype(jnp.bfloat16)

                @pl.when(me == part_)
                def _():
                    pltpu.make_async_copy(
                        o_stage.at[j, part_], out_ref.at[:, lanes], o_rsem
                    ).start()

                @pl.when(me != part_)
                def _():
                    pltpu.make_async_remote_copy(
                        src_ref=o_stage.at[j, part_],
                        dst_ref=out_ref.at[:, lanes],
                        send_sem=o_ssem.at[j],
                        recv_sem=o_rsem,
                        device_id=(blk, part_),
                        device_id_type=MESH,
                    ).start()

    def queries(j):
        exchange(q_stage, q_in, q_ssem, q_rsem, j)

    spread(0)
    queries(0)
    relay(0)
    spread(1)
    queries(1)
    forward(0)
    relay(1)
    spread(2)
    queries(2)
    forward(1)
    attend(0)
    relay(2)
    attend(1)
    forward(2)
    attend(2)

    sent = pl.ds(0, uly - 1)
    for j in range(heads_here):
        pltpu.make_async_copy(kv_in.at[j, sent], kv_in.at[j, sent], kv_ssem.at[j]).wait()
        pltpu.make_async_copy(q_in.at[j, sent], q_in.at[j, sent], q_ssem.at[j]).wait()
        to_other(j, 1).wait_send()
        sent_all(sides(j) + relays(j))
        sent_all(((has_left, to_other(j, 0)), (has_right, to_other(j, 2))))
        pltpu.make_async_copy(o_stage.at[j, sent], o_stage.at[j, sent], o_ssem.at[j]).wait()
    pltpu.make_async_copy(out_ref, out_ref, o_rsem).wait()


def on_device(cols, line, queries, keys, values, tile_pairs, tile_coords):
    uly = lax.axis_size("uly")
    chunk, columns = queries.shape
    heads_here = columns // HEAD_DIM // uly
    run = chunk * uly
    tiles = run // TILE
    vmem = pl.BlockSpec(memory_space=pltpu.VMEM)
    dma = pltpu.SemaphoreType.DMA
    bf16 = jnp.bfloat16
    heads = uly * heads_here
    window = pltpu.VMEM((3, 2 * tiles, 2, TILE, HEAD_DIM), bf16)
    return pl.pallas_call(
        functools.partial(kernel, uly, heads_here, cols, line),
        out_shape=jax.ShapeDtypeStruct(queries.shape, bf16),
        in_specs=[pl.BlockSpec(memory_space=pl.ANY)] * 5,
        out_specs=vmem,
        scratch_shapes=[
            pltpu.VMEM((heads, 2, chunk, HEAD_DIM), bf16),
            pltpu.VMEM((heads, chunk, HEAD_DIM), bf16),
            pltpu.VMEM((heads_here, uly, 2, chunk, HEAD_DIM), bf16),
            pltpu.VMEM((heads_here, uly, chunk, HEAD_DIM), bf16),
            window, window, window,
            pltpu.VMEM((tiles, TILE, HEAD_DIM), bf16),
            pltpu.VMEM((run, HEAD_DIM), jnp.float32),
            pltpu.VMEM((heads_here, uly, chunk, HEAD_DIM), bf16),
            dma((heads_here,)), dma((heads_here,)),
            dma((heads_here,)), dma((heads_here,)),
            dma((heads_here, 2, 2)), dma((heads_here, 2, 3)),
            dma((heads_here, 3)), dma((heads_here, 3)),
            dma((heads_here,)), dma(()),
            pltpu.VMEM((heads_here, 2, TILE, HEAD_DIM), bf16), dma((heads_here, 2)), dma((heads_here,)),
            pltpu.VMEM(queries.shape, bf16), pltpu.VMEM(queries.shape, bf16), pltpu.VMEM(queries.shape, bf16),
            pltpu.SMEM((16, KPT), jnp.int32), pltpu.SMEM((16, 3), jnp.int32), dma((5,)),
        ],
        compiler_params=pltpu.CompilerParams(
            collective_id=0, has_side_effects=True, vmem_limit_bytes=56 * 2 ** 20
        ),
    )(queries, keys, values, tile_pairs, tile_coords)


def solution(mesh):
    spec = P(("blk", "uly"), None)
    return jax.shard_map(
        functools.partial(on_device, mesh.shape["blk"] // 2, LINE),
        mesh=mesh,
        in_specs=(spec, spec, spec, P(), P()),
        out_specs=spec,
        check_vma=False,
    )
```

time: 83.9 us -> 75.1 us (0.90)
  the two profiles are of different devices: /device:TPU:46 before, /device:TPU:49 now
where the time goes in v2:
time: 75.1 us; the launch traced here: 74.9 us
  Pallas kernels  70.9 us (94%)
  local copies, waits for them, and re-layouts  4.03 us (5%)
    pallas_call x1, Pallas kernels, on_device(): pl.pallas_call(functools.partial(kernel, uly, heads_here, cols, line), ou...  70.9 us
    unnamed x5, local copies, waits for them, and re-layouts  4.03 us

profile of v2, /device:TPU:49, one launch (start us, length us, event | category | flops | bytes accessed | tf_op | source)
XLA Modules:
  0.0 74.9 jit_solution(760588799173385287)
XLA Ops:
  0.0 0.0 copy-start
  0.0 1.5 %copy.6.pairs_hbm = s32[192,8]{1,0:T(8,128)} copy(s32[192,8]{0,1:T(8,128)} %param.8) | data formatting | bytes 12288 | tf_op args[3]
  1.5 0.0 copy-done
  1.5 0.8 %copy.7.coords_hbm = s32[192,3]{1,0:T(8,128)} copy(s32[192,3]{0,1:T(4,128)S(1)} %copy-done) | data formatting | bytes 4608 | tf_op args[4]
  2.2 70.9 %shard_map.55 = bf16[72,3072]{1,0:T(8,128)(2,1)} custom-call(bf16[72,3072]{1,0:T(8,128)(2,1)} %q_hbm.1, bf16[72,3072]{1,0:T(8,128)(2,1)} %k_hbm.1, bf16[72,3072]{1,0:T(8,128)(2,1)} %v_hbm.1, s32[192,8]{1,0:T(8,128)} %copy.6.pairs_hbm, s32[192,3]{1,0:T(8,128)} %copy.7.coords_hbm), custom_call_target="tpu_custom_call" | custom-call | tf_op jit(solution)/shard_map/pallas_call | solution.py:462
  73.1 1.8 %copy.9 = bf16[72,3072]{1,0:T(8,128)(2,1)} copy(bf16[72,3072]{1,0:T(8,128)(2,1)} %shard_map.55) | data formatting | bytes 884736
Async XLA Ops:
  0.0 1.5 %copy-start = (s32[192,3]{0,1:T(4,128)S(1)}, s32[192,3]{0,1:T(4,128)}, u32[]{:S(2)}) copy-start(s32[192,3]{0,1:T(4,128)} %param.9) | copy-start | bytes 6916

commit v3 on v2

v3 whole, which is shorter than its diff:
```python
import functools
import math

import jax
import jax.numpy as jnp
from jax import lax
from jax.experimental import pallas as pl
from jax.experimental.pallas import tpu as pltpu
from jax.sharding import PartitionSpec as P

HEAD_DIM = 128
TF = 3
TH = 8
TW = 8
GF = 2
GH = 3
KPT = 8
TILE = 192
LINE = 8
MESH = pl.DeviceIdType.MESH
DIRECT = 0
SKIP = 4
BENDS = ((1, 0), (2, 1), (3, 2), (5, 5))


def rope_tables(coords, row, offset, count):
    shape = (count, HEAD_DIM)
    token = lax.broadcasted_iota(jnp.int32, shape, 0) + offset
    lane = lax.broadcasted_iota(jnp.int32, shape, 1)
    past = token >= TILE
    token = jnp.where(past, token - TILE, token)
    last = row + lax.div(offset + count - 1, TILE)

    def cell(axis):
        return jnp.where(past, coords[axis, last], coords[axis, row])

    halves = HEAD_DIM // 2
    side_pairs = HEAD_DIM // 6
    frame_pairs = halves - 2 * side_pairs
    pair = jnp.where(lane < halves, lane, lane - halves)
    in_frame = pair < frame_pairs
    in_height = pair < frame_pairs + side_pairs
    within = jnp.where(
        in_frame, pair, jnp.where(in_height, pair - frame_pairs, pair - frame_pairs - side_pairs)
    ).astype(jnp.float32)
    axis_len = jnp.where(in_frame, float(frame_pairs), float(side_pairs))
    frequency = jnp.exp(-math.log(10000.0) * within / axis_len)
    position = jnp.where(
        in_frame,
        cell(0) * TF + lax.div(token, TH * TW),
        jnp.where(
            in_height,
            cell(1) * TH + lax.rem(lax.div(token, TW), TH),
            cell(2) * TW + lax.rem(token, TW),
        ),
    ).astype(jnp.float32)
    angles = position * frequency
    return jnp.cos(angles), jnp.where(lane < halves, -jnp.sin(angles), jnp.sin(angles))


def kernel(
    uly, heads_here, cols, line,
    q_hbm, k_hbm, v_hbm, pairs_hbm, coords_hbm,
    out_ref,
    kv_stage, q_stage, kv_in, q_in, win0, win1, win2, q_rows, o_rows, o_stage,
    kv_ssem, kv_rsem, q_ssem, q_rsem, z_ssem, z_rsem, f_ssem, f_rsem, o_ssem, o_rsem,
    relay_buf, r_ssem, r_rsem, q_ref, k_ref, v_ref, pairs, coords, in_sem, go_sem,
):
    wins = (win0, win1, win2)
    heads = uly * heads_here
    chunk = q_ref.shape[0]
    run = chunk * uly
    blk = lax.axis_index("blk")
    me = lax.axis_index("uly")
    tiles = run // TILE
    loads = [
        pltpu.make_async_copy(src, dst, in_sem.at[n])
        for n, (src, dst) in enumerate((
            (coords_hbm, coords),
            (k_hbm, k_ref),
            (v_hbm, v_ref),
            (q_hbm, q_ref),
            (pairs_hbm, pairs),
        ))
    ]
    for load in loads:
        load.start()
    core = lax.rem(blk, 2)
    col = lax.div(blk, 2)
    has_left = col > 0
    has_right = col < cols - 1
    place = lax.rem(col, line)
    cross_left = (place == 0) & has_left
    cross_right = (place == line - 1) & has_right
    skip_right = (place == line - 2) & (col < cols - line)
    skip_left = (place == 1) & (col >= line)
    row = 2 * line
    span = row - 2
    bends = [
        (unit, (place == stop) & (col < cols - line), (place == line - 1 - stop) & (col >= line), 2 * stop)
        for unit, stop in BENDS
    ]
    peers = [lax.rem(me + step, uly) for step in (1, 3, 5, 7, 2, 6, 4)]
    other = blk + 1 - 2 * core

    barrier = pltpu.get_barrier_semaphore()
    for peer in peers:
        pl.semaphore_signal(barrier, inc=1, device_id=(blk - core, peer), device_id_type=MESH)
    pl.semaphore_signal(barrier, inc=1, device_id=(other, me), device_id_type=MESH)
    greeted = [
        (has_left, blk - 2),
        (has_right, blk + 2),
        (cross_left, blk - 4),
        (cross_right, blk + 4),
        (skip_right, blk + 4),
        (skip_left, blk - 4),
    ]
    for _, up, down, shift in bends:
        greeted += [
            (cross_left, blk + span - shift),
            (cross_left, blk - row + shift),
            (cross_right, blk - span + shift),
            (cross_right, blk + row - shift),
            (up, blk + span - shift),
            (up, blk + row - shift),
            (down, blk - span + shift),
            (down, blk - row + shift),
        ]
    columns_in = 0
    for due, target in greeted:
        columns_in = columns_in + due.astype(jnp.int32)

        @pl.when(due)
        def _():
            pl.semaphore_signal(
                barrier, inc=1, device_id=(target - core + 1, me), device_id_type=MESH
            )

    def tell_other():
        pl.semaphore_signal(go_sem, inc=1, device_id=(other, me), device_id_type=MESH)

    def wait_group():
        @pl.when(core == 0)
        def _():
            pl.semaphore_wait(barrier, 2 * (uly - 1) + 1)
            tell_other()

        @pl.when(core == 1)
        def _():
            pl.semaphore_wait(go_sem, 1)

    def wait_columns():
        @pl.when(core == 1)
        def _():
            pl.semaphore_wait(barrier, 2 * columns_in + 1)
            tell_other()

        @pl.when(core == 0)
        def _():
            pl.semaphore_wait(go_sem, 1)

    loads[0].wait()
    cosine, sine = rope_tables(
        coords,
        blk * tiles + lax.div(me * chunk, TILE),
        lax.rem(me * chunk, TILE),
        chunk,
    )

    def rotated(rows):
        rows = rows.astype(jnp.float32)
        return (rows * cosine + pltpu.roll(rows, HEAD_DIM // 2, 1) * sine).astype(jnp.bfloat16)

    def stage_kv(i, peer, carry):
        head = peer * heads_here + i // 2
        lanes = pl.ds(pl.multiple_of(head * HEAD_DIM, HEAD_DIM), HEAD_DIM)
        kv_stage[head, i % 2] = v_ref[:, lanes] if i % 2 else rotated(k_ref[:, lanes])
        return carry

    def stage_q(j, peer, carry):
        head = peer * heads_here + j
        lanes = pl.ds(pl.multiple_of(head * HEAD_DIM, HEAD_DIM), HEAD_DIM)
        q_stage[head] = rotated(q_ref[:, lanes])
        return carry

    def send(i):
        if i < 2:
            loads[1 + i].wait()
        lax.fori_loop(0, uly, functools.partial(stage_kv, i), 0)
        if i == 0:
            wait_group()
        exchange(lambda head: kv_stage.at[head, i % 2], kv_in.at[i], kv_ssem.at[i], kv_rsem.at[i], i // 2)

    def queries(j):
        if j == 0:
            loads[3].wait()
        lax.fori_loop(0, uly, functools.partial(stage_q, j), 0)
        exchange(lambda head: q_stage.at[head], q_in.at[j], q_ssem.at[j], q_rsem.at[j], j)

    def exchange(staged, landing, ssem, rsem, j):
        for peer in peers:
            pltpu.make_async_remote_copy(
                src_ref=staged(peer * heads_here + j),
                dst_ref=landing.at[me],
                send_sem=ssem,
                recv_sem=rsem,
                device_id=(blk, peer),
                device_id_type=MESH,
            ).start()
        pltpu.make_async_copy(staged(me * heads_here + j), landing.at[me], rsem).start()

    mine = pl.ds(core * tiles, tiles)
    theirs = pl.ds((1 - core) * tiles, tiles)

    def side(i, slot):
        return wins[i // 2].at[slot, i % 2]

    def to_other(i, slot):
        rows = side(i, slot).at[mine]
        return pltpu.make_async_remote_copy(
            src_ref=rows, dst_ref=rows, send_sem=f_ssem.at[i, slot], recv_sem=f_rsem.at[i, slot],
            device_id=(other, me), device_id_type=MESH,
        )

    def from_other(i, slot):
        rows = side(i, slot).at[theirs]
        return pltpu.make_async_copy(rows, rows, f_rsem.at[i, slot])

    def hop(src, dst, ssem, rsem, target):
        return pltpu.make_async_remote_copy(
            src_ref=src, dst_ref=dst, send_sem=ssem, recv_sem=rsem,
            device_id=(target, me), device_id_type=MESH,
        )

    last = tiles - 1

    def part(n):
        return core * tiles + last if n == 0 else pl.ds(core * tiles, last)

    def to_side(i, slot, target, n):
        return hop(
            side(i, 1).at[part(n)], side(i, 2 - slot).at[part(n)],
            z_ssem.at[i, slot // 2, n], z_rsem.at[i, 1 - slot // 2, n], target,
        )

    def unit(i, slot, n):
        rows = TILE // 2
        return side(i, slot).at[core * tiles + n // 2, pl.ds(n % 2 * rows, rows)]

    def direct(i, slot, target):
        return hop(
            unit(i, 1, DIRECT), unit(i, 2 - slot, DIRECT),
            z_ssem.at[i, slot // 2, 0], z_rsem.at[i, 1 - slot // 2, DIRECT], target,
        )

    def skip_out(i, slot, target):
        return hop(
            unit(i, slot, SKIP), unit(i, 2 - slot, SKIP),
            r_ssem.at[i, 6], z_rsem.at[i, 1 - slot // 2, SKIP], target,
        )

    def bend_in(i, n, which, way, target):
        return hop(
            unit(i, 1, n), relay_buf.at[i, way],
            r_ssem.at[i, which], r_rsem.at[i, way], target,
        )

    def bend_out(i, n, way, target):
        return hop(
            relay_buf.at[i, way], unit(i, 2 * way, n),
            r_ssem.at[i, 4 + way], z_rsem.at[i, way, n], target,
        )

    inner_right = has_right & ~cross_right
    inner_left = has_left & ~cross_left

    def sides(j):
        copies = []
        for which, (n, _, _, shift) in enumerate(bends):
            copies += [
                (cross_right, bend_in(j, n, which, 0, blk - span + shift)),
                (cross_left, bend_in(j, n, which, 1, blk + span - shift)),
            ]
        return copies + [
            (cross_right, direct(j, 2, blk + 2)),
            (cross_left, direct(j, 0, blk - 2)),
            (inner_right, to_side(j, 2, blk + 2, 0)),
            (inner_left, to_side(j, 0, blk - 2, 0)),
            (inner_right, to_side(j, 2, blk + 2, 1)),
            (inner_left, to_side(j, 0, blk - 2, 1)),
        ]

    def relays(j):
        copies = [
            (skip_right, skip_out(j, 2, blk + 4)),
            (skip_left, skip_out(j, 0, blk - 4)),
        ]
        for n, up, down, shift in bends:
            copies += [
                (up, bend_out(j, n, 0, blk + row - shift)),
                (down, bend_out(j, n, 1, blk - row + shift)),
            ]
        return copies

    def start_all(copies):
        for due, copy in copies:

            @pl.when(due)
            def _():
                copy.start()

    def sent_all(copies):
        for due, copy in copies:

            @pl.when(due)
            def _():
                copy.wait_send()

    def arrived(rows, sem):
        pltpu.make_async_copy(rows, rows, sem).wait()

    def gather_rows(landing, index, store):
        for pair in range(uly // 2):
            both = jnp.concatenate(
                [landing[index(2 * pair)].astype(jnp.float32), landing[index(2 * pair + 1)].astype(jnp.float32)],
                axis=0,
            ).astype(jnp.bfloat16)
            first, past = 2 * chunk * pair, 2 * chunk * (pair + 1)
            for tile in range(first // TILE, (past - 1) // TILE + 1):
                start, stop = max(first, tile * TILE), min(past, (tile + 1) * TILE)
                store(tile, start - tile * TILE, both[start - first : stop - first])

    def spread(j):
        arrived(kv_in.at[j], kv_rsem.at[j])

        def store(tile, row, value):
            wins[j // 2][1, j % 2, core * tiles + tile, pl.ds(row, value.shape[0])] = value

        gather_rows(kv_in, lambda s: (j, s), store)
        if j == 0:
            wait_columns()
        start_all(sides(j))
        to_other(j, 1).start()

    def relay(j):
        for _, up, down, _ in bends:
            for way, due in ((0, up), (1, down)):

                @pl.when(due)
                def _():
                    arrived(relay_buf.at[j, way], r_rsem.at[j, way])

        for slot, due in ((0, skip_left), (2, skip_right)):

            @pl.when(due)
            def _():
                arrived(side(j, slot).at[part(0)], z_rsem.at[j, slot // 2, 0])

        start_all(relays(j))

    def forward(j):
        for slot, inner, skips, cross in (
            (0, inner_left, skip_left, cross_left),
            (2, inner_right, skip_right, cross_right),
        ):

            @pl.when(inner)
            def _():
                @pl.when(~skips)
                def _():
                    arrived(side(j, slot).at[part(0)], z_rsem.at[j, slot // 2, 0])

                arrived(side(j, slot).at[part(1)], z_rsem.at[j, slot // 2, 1])
                to_other(j, slot).start()

            @pl.when(cross)
            def _():
                for n in range(2 * tiles):
                    arrived(unit(j, slot, n), z_rsem.at[j, slot // 2, n])
                to_other(j, slot).start()

    factor = HEAD_DIM ** -0.5 * math.log2(math.e)
    listed = KPT // 2

    def attend(j):
        pltpu.make_async_copy(q_in.at[j], q_in.at[j], q_rsem.at[j]).wait()
        def store(tile, row, value):
            q_rows[tile, pl.ds(row, value.shape[0])] = value
        gather_rows(q_in, lambda s: (j, s), store)
        for i in (2 * j, 2 * j + 1):
            from_other(i, 1).wait()

            @pl.when(has_left)
            def _():
                from_other(i, 0).wait()

            @pl.when(has_right)
            def _():
                from_other(i, 2).wait()

        lanes = pl.ds(pl.multiple_of((me * heads_here + j) * HEAD_DIM, HEAD_DIM), HEAD_DIM)
        for tile in range(tiles):
            side, first = choice[tile]

            def rows_of(slot, which):
                return jnp.concatenate(
                    [wins[j][slot, which, first + step] for step in range(listed)], axis=0
                )

            query = q_rows[tile]
            contract = (((1,), (1,)), ((), ()))
            near = lax.dot_general(
                query, rows_of(1, 0), contract, preferred_element_type=jnp.float32
            )
            far = lax.dot_general(
                query, rows_of(side, 0), contract, preferred_element_type=jnp.float32
            )
            largest = jnp.maximum(
                jnp.max(near, axis=1, keepdims=True), jnp.max(far, axis=1, keepdims=True)
            )
            near = jnp.exp2((near - largest) * factor)
            far = jnp.exp2((far - largest) * factor)
            total = jnp.sum(near, axis=1, keepdims=True) + jnp.sum(far, axis=1, keepdims=True)
            summed = jnp.dot(
                near.astype(jnp.bfloat16), rows_of(1, 1), preferred_element_type=jnp.float32
            ) + jnp.dot(
                far.astype(jnp.bfloat16), rows_of(side, 1), preferred_element_type=jnp.float32
            )
            o_rows[pl.ds(tile * TILE, TILE)] = summed / total
            for part_ in range(tile * TILE // chunk, (tile + 1) * TILE // chunk):
                o_stage[j, part_] = o_rows[pl.ds(part_ * chunk, chunk)].astype(jnp.bfloat16)

                @pl.when(me == part_)
                def _():
                    pltpu.make_async_copy(
                        o_stage.at[j, part_], out_ref.at[:, lanes], o_rsem
                    ).start()

                @pl.when(me != part_)
                def _():
                    pltpu.make_async_remote_copy(
                        src_ref=o_stage.at[j, part_],
                        dst_ref=out_ref.at[:, lanes],
                        send_sem=o_ssem.at[j],
                        recv_sem=o_rsem,
                        device_id=(blk, part_),
                        device_id_type=MESH,
                    ).start()

    choice = []

    def choose():
        loads[4].wait()

        for tile in range(tiles):
            here = blk * tiles + tile
            lowest = pairs[0, here]
            for slot in range(1, KPT):
                lowest = jnp.minimum(lowest, pairs[slot, here])
            across = lax.div(lowest, GF * GH)
            choice.append((
                jnp.where(across < col, 0, 2),
                jnp.clip(lowest - across * (GF * GH), 0, GF * GH - KPT // 2),
            ))

    sent = pl.ds(0, uly - 1)

    def left(like, ssem, j):
        pltpu.make_async_copy(like.at[j, sent], like.at[j, sent], ssem.at[j]).wait()

    send(0)
    send(1)
    choose()
    left(kv_in, kv_ssem, 0)
    send(2)
    spread(0)
    left(kv_in, kv_ssem, 1)
    send(3)
    spread(1)
    left(kv_in, kv_ssem, 2)
    send(4)
    relay(0)
    spread(2)
    left(kv_in, kv_ssem, 3)
    send(5)
    relay(1)
    forward(0)
    spread(3)
    left(kv_in, kv_ssem, 4)
    queries(0)
    relay(2)
    forward(1)
    spread(4)
    left(kv_in, kv_ssem, 5)
    queries(1)
    relay(3)
    forward(2)
    spread(5)
    left(q_in, q_ssem, 0)
    queries(2)
    relay(4)
    attend(0)
    forward(3)
    relay(5)
    attend(1)
    forward(4)
    forward(5)
    attend(2)
    for j in range(heads_here):
        if j == 1:
            left(q_in, q_ssem, j)
        if j == 2:
            left(q_in, q_ssem, j)
        left(o_stage, o_ssem, j)
    for i in range(2 * heads_here):
        to_other(i, 1).wait_send()
        sent_all(sides(i) + relays(i))
        sent_all(((has_left, to_other(i, 0)), (has_right, to_other(i, 2))))
    pltpu.make_async_copy(out_ref, out_ref, o_rsem).wait()


def on_device(cols, line, queries, keys, values, tile_pairs, tile_coords):
    uly = lax.axis_size("uly")
    chunk, columns = queries.shape
    heads_here = columns // HEAD_DIM // uly
    run = chunk * uly
    tiles = run // TILE
    vmem = pl.BlockSpec(memory_space=pltpu.VMEM)
    dma = pltpu.SemaphoreType.DMA
    bf16 = jnp.bfloat16
    heads = uly * heads_here
    window = pltpu.VMEM((3, 2, 2 * tiles, TILE, HEAD_DIM), bf16)
    stages = 2 * heads_here
    return pl.pallas_call(
        functools.partial(kernel, uly, heads_here, cols, line),
        out_shape=jax.ShapeDtypeStruct(queries.shape, bf16),
        in_specs=[pl.BlockSpec(memory_space=pltpu.HBM)] * 5,
        out_specs=vmem,
        scratch_shapes=[
            pltpu.VMEM((heads, 2, chunk, HEAD_DIM), bf16),
            pltpu.VMEM((heads, chunk, HEAD_DIM), bf16),
            pltpu.VMEM((stages, uly, chunk, HEAD_DIM), bf16),
            pltpu.VMEM((heads_here, uly, chunk, HEAD_DIM), bf16),
            window, window, window,
            pltpu.VMEM((tiles, TILE, HEAD_DIM), bf16),
            pltpu.VMEM((run, HEAD_DIM), jnp.float32),
            pltpu.VMEM((heads_here, uly, chunk, HEAD_DIM), bf16),
            dma((stages,)), dma((stages,)),
            dma((heads_here,)), dma((heads_here,)),
            dma((stages, 2, 2)), dma((stages, 2, 2 * tiles)),
            dma((stages, 3)), dma((stages, 3)),
            dma((heads_here,)), dma(()),
            pltpu.VMEM((stages, 2, TILE // 2, HEAD_DIM), bf16), dma((stages, 7)), dma((stages, 2)),
            pltpu.VMEM(queries.shape, bf16), pltpu.VMEM(queries.shape, bf16), pltpu.VMEM(queries.shape, bf16),
            pltpu.SMEM(tile_pairs.shape[::-1], jnp.int32), pltpu.SMEM(tile_coords.shape[::-1], jnp.int32), dma((5,)), pltpu.SemaphoreType.REGULAR,
        ],
        compiler_params=pltpu.CompilerParams(
            collective_id=0, has_side_effects=True, vmem_limit_bytes=56 * 2 ** 20
        ),
    )(queries, keys, values, tile_pairs.T, tile_coords.T)


def solution(mesh):
    spec = P(("blk", "uly"), None)
    return jax.shard_map(
        functools.partial(on_device, mesh.shape["blk"] // 2, LINE),
        mesh=mesh,
        in_specs=(spec, spec, spec, P(), P()),
        out_specs=spec,
        check_vma=False,
    )
```

time: 75.1 us -> 69.4 us (0.924)
  the two profiles are of different devices: /device:TPU:49 before, /device:TPU:63 now
where the time goes in v3:
time: 69.4 us; the launch traced here: 69.2 us
  Pallas kernels  67.4 us (97%)
  local copies, waits for them, and re-layouts  1.8 us (3%)
    pallas_call x1, Pallas kernels, on_device(): pl.pallas_call(functools.partial(kernel, uly, heads_here, cols, line), ou...  67.4 us
    unnamed x1, local copies, waits for them, and re-layouts  1.8 us

profile of v3, /device:TPU:63, one launch (start us, length us, event | category | flops | bytes accessed | tf_op | source)
XLA Modules:
  0.0 69.2 jit_solution(15778519277123571965)
XLA Ops:
  0.0 67.4 %shard_map.55 = bf16[72,3072]{1,0:T(8,128)(2,1)} custom-call(bf16[72,3072]{1,0:T(8,128)(2,1)} %q_hbm.1, bf16[72,3072]{1,0:T(8,128)(2,1)} %k_hbm.1, bf16[72,3072]{1,0:T(8,128)(2,1)} %v_hbm.1, s32[8,192]{1,0:T(8,128)} %bitcast.2, s32[3,192]{1,0:T(4,128)} %bitcast.3), custom_call_target="tpu_custom_call" | custom-call | tf_op jit(solution)/shard_map/pallas_call | solution.py:534
  67.4 1.8 %copy.7 = bf16[72,3072]{1,0:T(8,128)(2,1)} copy(bf16[72,3072]{1,0:T(8,128)(2,1)} %shard_map.55) | data formatting | bytes 884736

commit v4 on v3

--- a/solution.py
+++ b/solution.py
@@ -484,26 +484,26 @@
     left(kv_in, kv_ssem, 3)
     send(5)
     relay(1)
-    forward(0)
     spread(3)
     left(kv_in, kv_ssem, 4)
     queries(0)
     relay(2)
-    forward(1)
+    forward(0)
     spread(4)
     left(kv_in, kv_ssem, 5)
     queries(1)
     relay(3)
-    forward(2)
+    forward(1)
     spread(5)
     left(q_in, q_ssem, 0)
     queries(2)
     relay(4)
-    attend(0)
+    forward(2)
     forward(3)
     relay(5)
+    attend(0)
+    forward(4)
     attend(1)
-    forward(4)
     forward(5)
     attend(2)
     for j in range(heads_here):
@@ -535,7 +535,7 @@
         functools.partial(kernel, uly, heads_here, cols, line),
         out_shape=jax.ShapeDtypeStruct(queries.shape, bf16),
         in_specs=[pl.BlockSpec(memory_space=pltpu.HBM)] * 5,
-        out_specs=vmem,
+        out_specs=pl.BlockSpec(memory_space=pltpu.HBM),
         scratch_shapes=[
             pltpu.VMEM((heads, 2, chunk, HEAD_DIM), bf16),
             pltpu.VMEM((heads, chunk, HEAD_DIM), bf16),

time: 69.4 us -> 67.3 us (0.970)
  Pallas kernels: 67.4 us -> 65.3 us
    pallas_call x1, Pallas kernels: 67.4 us -> 65.3 us  [on_device(): pl.pallas_call(functools.partial(kernel, uly, heads_here, cols, line), ou...]
where the time goes in v4:
time: 67.3 us; the launch traced here: 67.1 us
  Pallas kernels  65.3 us (97%)
  local copies, waits for them, and re-layouts  1.8 us (3%)
    pallas_call x1, Pallas kernels, on_device(): pl.pallas_call(functools.partial(kernel, uly, heads_here, cols, line), ou...  65.3 us
    unnamed x1, local copies, waits for them, and re-layouts  1.8 us

profile of v4, /device:TPU:63, one launch (start us, length us, event | category | flops | bytes accessed | tf_op | source)
XLA Modules:
  0.0 67.1 jit_solution(4964442770885317952)
XLA Ops:
  0.0 65.3 %shard_map.55 = bf16[72,3072]{1,0:T(8,128)(2,1)} custom-call(bf16[72,3072]{1,0:T(8,128)(2,1)} %q_hbm.1, bf16[72,3072]{1,0:T(8,128)(2,1)} %k_hbm.1, bf16[72,3072]{1,0:T(8,128)(2,1)} %v_hbm.1, s32[8,192]{1,0:T(8,128)} %bitcast.2, s32[3,192]{1,0:T(4,128)} %bitcast.3), custom_call_target="tpu_custom_call" | custom-call | tf_op jit(solution)/shard_map/pallas_call | solution.py:534
  65.3 1.8 %copy.7 = bf16[72,3072]{1,0:T(8,128)(2,1)} copy(bf16[72,3072]{1,0:T(8,128)(2,1)} %shard_map.55) | data formatting | bytes 884736

commit v5 on v4

--- a/solution.py
+++ b/solution.py
@@ -94,6 +94,7 @@
     cross_right = (place == line - 1) & has_right
     skip_right = (place == line - 2) & (col < cols - line)
     skip_left = (place == 1) & (col >= line)
+    early = place < 3
     row = 2 * line
     span = row - 2
     bends = [
@@ -343,20 +344,23 @@
         to_other(j, 1).start()
 
     def relay(j):
-        for _, up, down, _ in bends:
-            for way, due in ((0, up), (1, down)):
-
-                @pl.when(due)
-                def _():
-                    arrived(relay_buf.at[j, way], r_rsem.at[j, way])
-
-        for slot, due in ((0, skip_left), (2, skip_right)):
-
+        def pass_on(due, rows, sem, copy):
             @pl.when(due)
             def _():
-                arrived(side(j, slot).at[part(0)], z_rsem.at[j, slot // 2, 0])
-
-        start_all(relays(j))
+                arrived(rows, sem)
+                copy.start()
+
+        for way, skips, skip in (
+            (1, skip_left, skip_out(j, 0, blk - 4)),
+            (0, skip_right, skip_out(j, 2, blk + 4)),
+        ):
+            for n, up, down, shift in bends:
+                target = blk - row + shift if way else blk + row - shift
+                pass_on(
+                    down if way else up, relay_buf.at[j, way], r_rsem.at[j, way],
+                    bend_out(j, n, way, target),
+                )
+            pass_on(skips, side(j, 2 - 2 * way).at[part(0)], z_rsem.at[j, 1 - way, 0], skip)
 
     def forward(j):
         for slot, inner, skips, cross in (
@@ -479,10 +483,17 @@
     spread(1)
     left(kv_in, kv_ssem, 2)
     send(4)
-    relay(0)
+    @pl.when(~early)
+    def _():
+        relay(0)
+
     spread(2)
     left(kv_in, kv_ssem, 3)
     send(5)
+    @pl.when(early)
+    def _():
+        relay(0)
+
     relay(1)
     spread(3)
     left(kv_in, kv_ssem, 4)
@@ -499,9 +510,16 @@
     queries(2)
     relay(4)
     forward(2)
+    @pl.when(early)
+    def _():
+        attend(0)
+
     forward(3)
     relay(5)
-    attend(0)
+    @pl.when(~early)
+    def _():
+        attend(0)
+
     forward(4)
     attend(1)
     forward(5)

time: 67.3 us -> 67 us (level)
  no operation moved by 1% of the time
where the time goes in v5:
time: 67 us; the launch traced here: 66.8 us
  Pallas kernels  65 us (97%)
  local copies, waits for them, and re-layouts  1.8 us (3%)
    pallas_call x1, Pallas kernels, on_device(): pl.pallas_call(functools.partial(kernel, uly, heads_here, cols, line), ou...  65 us
    unnamed x1, local copies, waits for them, and re-layouts  1.8 us

profile of v5, /device:TPU:63, one launch (start us, length us, event | category | flops | bytes accessed | tf_op | source)
XLA Modules:
  0.0 66.8 jit_solution(5391854975563613026)
XLA Ops:
  0.0 65.0 %shard_map.55 = bf16[72,3072]{1,0:T(8,128)(2,1)} custom-call(bf16[72,3072]{1,0:T(8,128)(2,1)} %q_hbm.1, bf16[72,3072]{1,0:T(8,128)(2,1)} %k_hbm.1, bf16[72,3072]{1,0:T(8,128)(2,1)} %v_hbm.1, s32[8,192]{1,0:T(8,128)} %bitcast.2, s32[3,192]{1,0:T(4,128)} %bitcast.3), custom_call_target="tpu_custom_call" | custom-call | tf_op jit(solution)/shard_map/pallas_call | solution.py:552
  65.0 1.8 %copy.7 = bf16[72,3072]{1,0:T(8,128)(2,1)} copy(bf16[72,3072]{1,0:T(8,128)(2,1)} %shard_map.55) | data formatting | bytes 884736

commit v6 on v5

--- a/solution.py
+++ b/solution.py
@@ -187,15 +187,19 @@
     def send(i):
         if i < 2:
             loads[1 + i].wait()
-        lax.fori_loop(0, uly, functools.partial(stage_kv, i), 0)
+            lax.fori_loop(0, uly, functools.partial(stage_kv, i), 0)
         if i == 0:
             wait_group()
         exchange(lambda head: kv_stage.at[head, i % 2], kv_in.at[i], kv_ssem.at[i], kv_rsem.at[i], i // 2)
 
+    def stage_rest():
+        for i in range(2, 2 * heads_here):
+            lax.fori_loop(0, uly, functools.partial(stage_kv, i), 0)
+        loads[3].wait()
+        for j in range(heads_here):
+            lax.fori_loop(0, uly, functools.partial(stage_q, j), 0)
+
     def queries(j):
-        if j == 0:
-            loads[3].wait()
-        lax.fori_loop(0, uly, functools.partial(stage_q, j), 0)
         exchange(lambda head: q_stage.at[head], q_in.at[j], q_ssem.at[j], q_rsem.at[j], j)
 
     def exchange(staged, landing, ssem, rsem, j):
@@ -474,6 +478,7 @@
 
     send(0)
     send(1)
+    stage_rest()
     choose()
     left(kv_in, kv_ssem, 0)
     send(2)

time: 67 us -> 67.8 us (1.012)
  the two profiles are of different devices: /device:TPU:63 before, /device:TPU:25 now
where the time goes in v6:
time: 67.8 us; the launch traced here: 67.6 us
  Pallas kernels  65.8 us (97%)
  local copies, waits for them, and re-layouts  1.8 us (3%)
    pallas_call x1, Pallas kernels, on_device(): pl.pallas_call(functools.partial(kernel, uly, heads_here, cols, line), ou...  65.8 us
    unnamed x1, local copies, waits for them, and re-layouts  1.8 us

profile of v6, /device:TPU:25, one launch (start us, length us, event | category | flops | bytes accessed | tf_op | source)
XLA Modules:
  0.0 67.6 jit_solution(16448523458176087854)
XLA Ops:
  0.0 65.8 %shard_map.55 = bf16[72,3072]{1,0:T(8,128)(2,1)} custom-call(bf16[72,3072]{1,0:T(8,128)(2,1)} %q_hbm.1, bf16[72,3072]{1,0:T(8,128)(2,1)} %k_hbm.1, bf16[72,3072]{1,0:T(8,128)(2,1)} %v_hbm.1, s32[8,192]{1,0:T(8,128)} %bitcast.2, s32[3,192]{1,0:T(4,128)} %bitcast.3), custom_call_target="tpu_custom_call" | custom-call | tf_op jit(solution)/shard_map/pallas_call | solution.py:557
  65.8 1.8 %copy.7 = bf16[72,3072]{1,0:T(8,128)(2,1)} copy(bf16[72,3072]{1,0:T(8,128)(2,1)} %shard_map.55) | data formatting | bytes 884736
